TPU v7x, 512 devices: a whole 4x4x16 slice. The times are simulated.
512 devices in a mesh: enc: 8 (over x, z_hi), ctx: 8 (over y, core), head: 8 (over z_lo).
Axes of the slice: x: 4, y: 4, z: 16 (z_hi: 2, z_lo: 8; z = z_hi * 8 + z_lo), core: 2. Of those that a mesh axis runs over, the one named last changes fastest.
Arguments:
- text_rows: bfloat16 [65536, 8, 768], P(('enc', 'ctx', 'head')), may hold values from -16 to 16
- vision_rows: bfloat16 [32768, 8, 768], P(('enc', 'ctx'), 'head'), may hold values from -6 to 6
- vision_pos: int32 [32768], replicated, may hold values from 0 to 65535, as said below
- doc_ids: int32 [65536], P(('enc', 'ctx')), may hold values from 0 to 511, never falling along the last dimension, each value on 1 to 256 neighbouring positions
Outputs:
- attended: bfloat16 [65536, 8, 512], P(('enc', 'ctx', 'head'))
Inputs may be any that keep to these rules, and one draw needn't show every extreme that they name: `vision_pos`: the positions are distinct. Entries k * 512 to (k + 1) * 512 - 1 are the rows of encoder group k (in the order of enc+ctx) and rise. At most 16 rows of one group lie among the 1024 positions m * 1024 to (m + 1) * 1024 - 1 of one context shard; in every draw some context shard receives exactly 16 rows from every group.
All inputs are finite; a program needn't handle non-finite values.
Results may differ from a plain program's by a relative error of at most 0.0032.
Values may be sent and summed in bfloat16 or wider, within the bound.
No kernel may reach another device: no remote copies, remote signals or barrier semaphores. Data moves between devices by JAX's collectives and lax.ppermute only.
A program may use at most 64 MiB of HBM per device.

v0:
```python
import jax
import jax.numpy as jnp
from jax import lax
from jax.sharding import PartitionSpec as P

HD = 128
QPG = 4


def from_behind(value, axis, steps):
    count = lax.axis_size(axis)
    initial, last = (max(0, -steps), min(count, count - steps))
    return lax.ppermute(value, axis, [(source, source + steps) for source in range(initial, last)])


def attend_block(queries, key_rows, value_rows, query_docs, key_docs, offset, factor):
    scores = (
        jnp.einsum("qghd,kgd->ghqk", queries, key_rows, preferred_element_type=jnp.float32) * factor
    )
    query_pos = offset + jnp.arange(queries.shape[0], dtype=jnp.int32)
    key_pos = jnp.arange(key_rows.shape[0], dtype=jnp.int32)
    allowed = (key_docs[None, :] == query_docs[:, None]) & (key_pos[None, :] <= query_pos[:, None])
    masked = jnp.where(allowed, scores, -jnp.inf)
    row_max = jnp.max(masked, axis=-1, keepdims=True)
    expo_terms = jnp.where(allowed, jnp.exp(masked - row_max), 0.0)
    row_total = jnp.sum(expo_terms, axis=-1)
    weights = expo_terms.astype(jnp.bfloat16)
    summed = jnp.einsum("ghqk,kgd->qghd", weights, value_rows, preferred_element_type=jnp.float32)
    return summed / jnp.transpose(row_total, (2, 0, 1))[..., None]


def body(text_rows, vision_rows, vision_pos, doc_ids):
    regrouped = lax.all_to_all(text_rows, "head", split_axis=1, concat_axis=0, tiled=True)
    shard_rows = regrouped.shape[0]
    groups = regrouped.shape[1]
    row_width = regrouped.shape[2]
    sources = lax.axis_size(("enc", "ctx"))
    slot_count = shard_rows // sources
    per_group = vision_rows.shape[0]
    source_id = lax.axis_index(("enc", "ctx"))
    target_shard = vision_pos // shard_rows
    own_targets = lax.dynamic_slice_in_dim(target_shard, source_id * per_group, per_group)
    shard_ids = jnp.arange(sources, dtype=jnp.int32)
    first_row = jnp.sum((own_targets[:, None] < shard_ids[None, :]).astype(jnp.int32), axis=0)
    row_counts = jnp.sum((own_targets[:, None] == shard_ids[None, :]).astype(jnp.int32), axis=0)
    slot_index = jnp.arange(slot_count, dtype=jnp.int32)
    source_row = jnp.clip(first_row[:, None] + slot_index[None, :], 0, per_group - 1)
    occupied = slot_index[None, :] < row_counts[:, None]
    outgoing = jnp.where(
        occupied[:, :, None, None], vision_rows[source_row], jnp.zeros((), vision_rows.dtype)
    )
    arrived = lax.all_to_all(outgoing, ("enc", "ctx"), split_axis=0, concat_axis=0, tiled=True)
    arrived = arrived.reshape(sources * slot_count, groups, row_width)
    by_source = target_shard.reshape(sources, per_group)
    skip_rows = jnp.sum((by_source < source_id).astype(jnp.int32), axis=1)
    arriving = jnp.sum((by_source == source_id).astype(jnp.int32), axis=1)
    lookup = shard_ids[:, None] * per_group + skip_rows[:, None] + slot_index[None, :]
    present = slot_index[None, :] < arriving[:, None]
    landing = jnp.where(
        present,
        vision_pos[jnp.clip(lookup, 0, vision_pos.shape[0] - 1)] - source_id * shard_rows,
        shard_rows,
    )
    total_slots = sources * slot_count
    slot_of_row = (
        jnp.full((shard_rows,), total_slots, jnp.int32)
        .at[landing.reshape(-1)]
        .set(jnp.arange(total_slots, dtype=jnp.int32), mode="drop")
    )
    merged = jnp.where(
        (slot_of_row < total_slots)[:, None, None],
        arrived[jnp.clip(slot_of_row, 0, total_slots - 1)],
        regrouped,
    )
    query_width = QPG * HD
    key_values = merged[:, :, query_width:]
    doc_marks = doc_ids + 1
    reach = shard_rows // 4
    prior_kv, prior_marks = from_behind(
        (key_values[shard_rows - reach :], doc_marks[shard_rows - reach :]), ("enc", "ctx"), 1
    )
    joined_kv = jnp.concatenate([prior_kv, key_values], 0)
    joined_marks = jnp.concatenate([prior_marks, doc_marks], 0)
    block_rows = shard_rows // 2
    factor = HD ** (-0.5)
    pieces = []
    for portion in range(2):
        low_row = portion * block_rows
        queries = merged[low_row : low_row + block_rows, :, :query_width].reshape(
            block_rows, groups, QPG, HD
        )
        window = joined_kv[low_row : low_row + reach + block_rows]
        window_marks = joined_marks[low_row : low_row + reach + block_rows]
        attended = attend_block(
            queries,
            window[:, :, :HD],
            window[:, :, HD:],
            doc_marks[low_row : low_row + block_rows],
            window_marks,
            reach,
            factor,
        )
        pieces.append(attended.reshape(block_rows, groups, query_width).astype(jnp.bfloat16))
    result = jnp.concatenate(pieces, 0)
    return lax.all_to_all(result, "head", split_axis=0, concat_axis=1, tiled=True)


def solution(mesh):
    in_specs = (
        P(("enc", "ctx", "head"), None, None),
        P(("enc", "ctx"), "head", None),
        P(),
        P(("enc", "ctx")),
    )
    out_specs = P(("enc", "ctx", "head"), None, None)
    return jax.shard_map(body, mesh=mesh, in_specs=in_specs, out_specs=out_specs, check_vma=False)
```

profile of v0, /device:TPU:1, one launch (start us, length us, event | category | flops | bytes accessed | tf_op | source)
XLA Modules:
  0.0 297.5 jit_solution(4788225846345836732)
XLA Ops:
  1.5 4.0 %gather_fusion.1 = bf16[1024,768]{1,0:T(8,128)(2,1)S(1)} fusion(bf16[512,768]{1,0:T(8,128)(2,1)S(1)} %bitcast.126, s32[1024]{0:T(1024)S(1)} %broadcast_clamp_fusion), kind=kCustom, calls=%fused_computation.1 | custom fusion | bytes 3149824 | tf_op jit(solution)/shard_map/gather | solution.py:50
  6.9 22.2 %all-to-all-start = ((bf16[64,16,1,768]{3,1,2,0:T(8,128)(2,1)}), bf16[64,16,1,768]{3,1,2,0:T(8,128)(2,1)S(1)}, u32[]{:S(2)}, u32[]{:S(2)}) async-start(bf16[64,16,1,768]{3,1,2,0:T(8,128)(2,1)} %broadcast_select_fusion), calls=%async_computation | async-start | bytes 3145728 | tf_op jit(solution)/shard_map/all_to_all | solution.py:52
  29.2 2.9 copy.35
  32.0 39.2 %all-to-all-done = bf16[64,16,1,768]{3,1,2,0:T(8,128)(2,1)S(1)} async-done(((bf16[64,16,1,768]{3,1,2,0:T(8,128)(2,1)}), bf16[64,16,1,768]{3,1,2,0:T(8,128)(2,1)S(1)}, u32[]{:S(2)}, u32[]{:S(2)}) %all-to-all-start) | async-done | bytes 1572896 | tf_op jit(solution)/shard_map/all_to_all | solution.py:52
  71.2 45.1 %all-to-all-start.1 = ((bf16[128,8,768]{2,0,1:T(8,128)(2,1)}), bf16[128,8,768]{2,0,1:T(8,128)(2,1)}, u32[]{:S(2)}, u32[]{:S(2)}) async-start(bf16[128,8,768]{2,0,1:T(8,128)(2,1)} %copy.35), calls=%async_computation.1 | async-start | bytes 3145728 | tf_op jit(solution)/shard_map/all_to_all | solution.py:33
  116.3 3.1 %collective-permute-start.1 = (s32[256]{0:T(256)S(1)}, s32[256]{0:T(256)S(1)}, u32[]{:S(2)}, u32[]{:S(2)}) collective-permute-start(s32[256]{0:T(256)S(1)} %slice.50), channel_id=1, source_target_pairs={{0,8},{8,16},{16,24},{24,32},{32,40},{40,48},{48,56},{56,64},{64,7... | collective-permute-start | bytes 3080 | tf_op jit(solution)/shard_map/ppermute | solution.py:13
  119.9 6.2 %gather_fusion = s32[1024]{0:T(1024)S(1)} fusion(s32[32768]{0:T(1024)S(1)} %copy-done.1, s32[1024]{0:T(1024)S(1)} %broadcast_clamp_fusion.1), kind=kCustom, calls=%fused_computation | custom fusion | bytes 12288 | tf_op jit(solution)/shard_map/gather | solution.py:61
  126.5 4.3 %scatter_custom_fusion = s32[1024]{0:T(1024)S(1)} fusion(s32[1024]{0:T(1024)S(1)} %bitcast.135, s32[1024]{0:T(1024)S(1)} %iota.39, s32[]{:T(128)} %constant.19.clone.1), kind=kCustom, calls=%fused_computation.69 | custom fusion | bytes 4100 | tf_op jit(solution)/shard_map/scatter | solution.py:68
  132.3 5.2 %gather_fusion.2 = bf16[1024,768]{1,0:T(8,128)(2,1)} fusion(bf16[1024,768]{1,0:T(8,128)(2,1)S(1)} %bitcast.127, s32[1024]{0:T(1024)S(1)} %fusion.37), kind=kCustom, calls=%fused_computation.2 | custom fusion | bytes 3149824 | tf_op jit(solution)/shard_map/gather | solution.py:72
  137.5 52.2 %all-to-all-done.1 = bf16[128,8,768]{2,0,1:T(8,128)(2,1)} async-done(((bf16[128,8,768]{2,0,1:T(8,128)(2,1)}), bf16[128,8,768]{2,0,1:T(8,128)(2,1)}, u32[]{:S(2)}, u32[]{:S(2)}) %all-to-all-start.1) | async-done | bytes 1572896 | tf_op jit(solution)/shard_map/all_to_all | solution.py:33
  189.7 2.1 bitcast_select_fusion.2
  192.7 2.1 collective-permute-start
  195.7 5.0 %fusion.1 = (f32[4,512]{1,0:T(4,128)S(1)}, f32[768,512,4]{1,0,2:T(8,128)}) fusion(pred[512,768]{0,1:T(8,128)(4,1)} %get-tuple-element.16, bf16[512,4,128]{2,1,0:T(4,128)(2,1)} %reshape.320, bf16[1024,1,768]{2,0,1:T(8,128)(2,1)S(1)} %bitcast_select_fusion.2), kind=kOutput, calls=%fused_computation.9 | convolution fusion | flops 407369728 | bytes 7413760 | tf_op jit(solution)/shard_map/qghd,kgd->ghqk/dot_general | solution.py:18
  200.8 2.1 copy.36
  202.8 2.3 fusion
  205.8 3.1 %fusion.2 = (f32[4,512]{1,0:T(4,128)S(1)}, f32[4,512]{1,0:T(4,128)S(1)}) fusion(f32[768,512,4]{1,0,2:T(8,128)S(1)} %get-tuple-element.20, f32[4,512]{1,0:T(4,128)S(1)} %get-tuple-element.19, pred[512,768]{0,1:T(8,128)(4,1)S(1)} %get-tuple-element.15, f32[4,512]{1,0:T(4,128)S(1)} %get-tuple-element.17, f32[768,512,4]{1,0,2:T(8,128)S(1)} %copy-done.2, ...), kind=kLoop, calls=%fused_computation.10 | loop fusion | flops 15724544 | bytes 13402112 | tf_op jit(solution)/shard_map/reduce_sum | solution.py:26
  208.9 2.5 divide_convert_fusion.1
  211.4 3.6 %copy.43 = bf16[512,1,512]{2,1,0:T(2,128)(2,1)} copy(bf16[512,1,512]{0,2,1:T(8,128)(2,1)} %bitcast.131) | data formatting | bytes 1048576 | tf_op jit(solution)/shard_map/convert_element_type | solution.py:103
  215.0 4.5 %divide_convert_fusion = bf16[512,1,4,128]{0,3,2,1:T(8,128)(2,1)S(1)} fusion(f32[768,512,4]{1,0,2:T(8,128)} %get-tuple-element.18, f32[4,512]{1,0:T(4,128)S(1)} %get-tuple-element.17, pred[512,768]{0,1:T(8,128)(4,1)} %get-tuple-element.16, f32[512,4]{0,1:T(4,128)S(1)} %bitcast.133, bf16[1024,1,768]{2,0,1:T(8,128)(2,1)S(1)} %bitcast_select_fusion.2), kind=kOutput, calls=%fused_computation.28 | convolution fusion | flops 411041792 | bytes 7421952 | tf_op jit(solution)/shard_map/ghqk,kgd->qghd/dot_general | solution.py:28
  219.6 2.0 copy.44
  221.6 4.2 %pad_maximum_fusion = bf16[1024,1,512]{2,1,0:T(2,128)(2,1)S(1)} fusion(bf16[512,1,512]{2,1,0:T(2,128)(2,1)} %copy.44, bf16[512,1,512]{2,1,0:T(2,128)(2,1)} %copy.43), kind=kLoop, calls=%fused_computation.20 | loop fusion | flops 524288 | bytes 2097152 | tf_op jit(solution)/shard_map/concatenate | solution.py:104
  226.4 8.1 %reduce.4 = bf16[1024,512]{1,0:T(8,128)(2,1)} reduce(bf16[1024,1,512]{2,1,0:T(2,128)(2,1)S(1)} %pad_maximum_fusion, bf16[]{:T(256)} %broadcast.299), dimensions={1}, to_apply=%pad_maximum_fusion.reduce_sub_computation | reduce | bytes 2097154 | tf_op jit(solution)/shard_map/concatenate | solution.py:104
  236.3 55.0 %all_to_all.41 = bf16[8,2,32768]{2,1,0:T(2,128)(2,1)} all-to-all(bf16[8,2,32768]{2,1,0:T(2,128)(2,1)S(1)} %reshape.373), channel_id=1, replica_groups=mesh['enc'=8,'ctx'=8,'head'=8] {'head'}, dimensions={0} | all-to-all | bytes 2097152 | tf_op jit(solution)/shard_map/all_to_all | solution.py:105
  291.3 4.3 %reshape.374 = bf16[1024,1,512]{2,1,0:T(2,128)(2,1)S(1)} reshape(bf16[8,2,32768]{2,1,0:T(2,128)(2,1)} %all_to_all.41) | data formatting | bytes 2097152
  (51 shorter events, 11.9 us)
Async XLA Ops:
  0.0 1.5 copy-start
  5.5 110.7 %copy-start.4 = (s32[1024]{0:T(1024)S(1)}, s32[1024]{0:T(1024)}, u32[]{:S(2)}) copy-start(s32[1024]{0:T(1024)} %param.7) | copy-start | bytes 12292
  5.6 113.9 %copy-start.1 = (s32[32768]{0:T(1024)S(1)}, s32[32768]{0:T(1024)}, u32[]{:S(2)}) copy-start(s32[32768]{0:T(1024)} %param.6) | copy-start | bytes 393220
  6.9 64.3 %all-to-all-start = ((bf16[64,16,1,768]{3,1,2,0:T(8,128)(2,1)}), bf16[64,16,1,768]{3,1,2,0:T(8,128)(2,1)S(1)}, u32[]{:S(2)}, u32[]{:S(2)}) async-start(bf16[64,16,1,768]{3,1,2,0:T(8,128)(2,1)} %broadcast_select_fusion), calls=%async_computation | async-start | bytes 3145728 | tf_op jit(solution)/shard_map/all_to_all | solution.py:52
  71.2 118.5 %all-to-all-start.1 = ((bf16[128,8,768]{2,0,1:T(8,128)(2,1)}), bf16[128,8,768]{2,0,1:T(8,128)(2,1)}, u32[]{:S(2)}, u32[]{:S(2)}) async-start(bf16[128,8,768]{2,0,1:T(8,128)(2,1)} %copy.35), calls=%async_computation.1 | async-start | bytes 3145728 | tf_op jit(solution)/shard_map/all_to_all | solution.py:33
  116.3 14.5 %collective-permute-start.1 = (s32[256]{0:T(256)S(1)}, s32[256]{0:T(256)S(1)}, u32[]{:S(2)}, u32[]{:S(2)}) collective-permute-start(s32[256]{0:T(256)S(1)} %slice.50), channel_id=1, source_target_pairs={{0,8},{8,16},{16,24},{24,32},{32,40},{40,48},{48,56},{56,64},{64,7... | collective-permute-start | bytes 3080 | tf_op jit(solution)/shard_map/ppermute | solution.py:13
  192.7 10.1 %collective-permute-start = (bf16[256,1,256]{2,0,1:T(8,128)(2,1)S(1)}, bf16[256,1,256]{2,0,1:T(8,128)(2,1)S(1)}, u32[]{:S(2)}, u32[]{:S(2)}) collective-permute-start(bf16[256,1,256]{2,0,1:T(8,128)(2,1)S(1)} %slice.66), channel_id=1, source_target_pairs={{0,8},{8,16},{16,24},{24,32},{32,40},{40,48},{48,56},{56,64},{64,7... | collective-permute-start | bytes 393224 | tf_op jit(solution)/shard_map/ppermute | solution.py:13
  202.8 2.9 copy-start.2
  202.8 3.0 copy-start.3
where the time goes:
time: 298 us; the launch traced here: 297 us
  waiting for transfers between devices  91.4 us (31%)
  starting transfers between devices  72.5 us (24%)
  blocking collectives  55 us (18%)
  local copies, waits for them, and re-layouts  41.7 us (14%)
  other arithmetic  22.2 us (7%)
  matrix products  14.4 us (5%)
    all_to_all x1, blocking collectives, body(): lax.all_to_all(result, 'head', split_axis=0, concat_axis=1, tiled=True)  55 us
    all_to_all x1, waiting for transfers between devices, body(): lax.all_to_all(text_rows, 'head', split_axis=1, concat_axis=0, tiled=True)  52.2 us
    all_to_all x1, starting transfers between devices, body(): lax.all_to_all(text_rows, 'head', split_axis=1, concat_axis=0, tiled=True)  45.1 us
    all_to_all x1, waiting for transfers between devices, body(): lax.all_to_all(outgoing, ('enc', 'ctx'), split_axis=0, concat_axis=0, til...  39.2 us
    all_to_all x1, starting transfers between devices, body(): lax.all_to_all(outgoing, ('enc', 'ctx'), split_axis=0, concat_axis=0, til...  22.2 us
    concatenate x2, other arithmetic, body(): result = jnp.concatenate(pieces, 0)  12.3 us
    unnamed x14, local copies, waits for them, and re-layouts  9.92 us
    dot_general x2, matrix products, attend_block(): jnp.einsum('qghd,kgd->ghqk', queries, key_rows, preferred_element_type=jn...  7.32 us
  transfers between devices with their start and end apart: 4, of which 2 were waited for; matrix products, arithmetic and copies ran while one was open for 10% of the time, Pallas kernels for 0%

commit v1 on v0

v1 whole, which is shorter than its diff:
```python
import functools

import jax
import jax.numpy as jnp
from jax import lax
from jax.experimental import pallas as pl
from jax.experimental.pallas import tpu as pltpu
from jax.sharding import Mesh
from jax.sharding import PartitionSpec as P

HD = 128
QPG = 4
GROUPS = 8
QW = QPG * HD
KW = 2 * HD
ROWS = 128
SHARD = 1024
SLOTS = 16
PER_SOURCE = 512
REACH = 256
AXES = ("x", "zh", "y", "c", "zl")
SIZES = (4, 2, 4, 2, 8)
COUNT = 512
VMEM = 48 * 1024 * 1024


def flat_id(x, zh, y, c, zl):
    return (((x * 2 + zh) * 4 + y) * 2 + c) * 8 + zl


def pairs(move):
    ids = []
    for x in range(4):
        for zh in range(2):
            for y in range(4):
                for c in range(2):
                    for zl in range(8):
                        ids.append((flat_id(x, zh, y, c, zl), flat_id(*move(x, zh, y, c, zl))))
    return ids


def to_other_half(value):
    return lax.ppermute(value, AXES, pairs(lambda x, zh, y, c, zl: (x, 1 - zh, y, c, zl)))


def along_head(value, steps):
    return lax.ppermute(value, AXES, pairs(lambda x, zh, y, c, zl: (x, zh, y, c, (zl + steps) % 8)))


def from_behind(value, steps):
    return lax.ppermute(value, AXES, [(i, i + steps) for i in range(COUNT - steps)])


def over_columns(slots):
    width = slots.shape[-1]
    swapped = lax.all_to_all(
        slots.reshape(32, SLOTS, width), ("x", "y", "c"), split_axis=0, concat_axis=0, tiled=True
    )
    return swapped.reshape(32 * SLOTS, width)


def onehot_rows(first, codes):
    rows = lax.broadcasted_iota(jnp.int32, (ROWS, codes.shape[1]), 0) + first
    return jnp.where(rows == codes, 1.0, 0.0).astype(jnp.bfloat16)


def slots_kernel(code_ref, rows_ref, out_ref):
    for part in range(PER_SOURCE // ROWS):
        pick = onehot_rows(part * ROWS, code_ref[...])
        placed = jnp.dot(pick, rows_ref[...], preferred_element_type=jnp.float32)
        out_ref[part * ROWS : (part + 1) * ROWS, :] = placed.astype(jnp.bfloat16)


def vmem():
    return pl.BlockSpec(memory_space=pltpu.VMEM)


def smem():
    return pl.BlockSpec(memory_space=pltpu.SMEM)


def params():
    return pltpu.CompilerParams(vmem_limit_bytes=VMEM)


def to_slots(code, rows):
    return pl.pallas_call(
        slots_kernel,
        out_shape=jax.ShapeDtypeStruct((PER_SOURCE, rows.shape[1]), jnp.bfloat16),
        in_specs=[vmem(), vmem()],
        out_specs=vmem(),
        compiler_params=params(),
        name="to_slots",
    )(code, rows)


def blocks_kernel(low, high, zl_ref, near_code, far_code, near_ref, far_ref, *outs):
    zl = zl_ref[0]
    for step in range(GROUPS):
        first = lax.rem(zl + step, GROUPS) * ROWS
        near = jnp.dot(
            onehot_rows(first, near_code[...]),
            near_ref[:, low:high],
            preferred_element_type=jnp.float32,
        )
        far = jnp.dot(
            onehot_rows(first, far_code[...]), far_ref[...], preferred_element_type=jnp.float32
        )
        outs[step][...] = (near + far).astype(jnp.bfloat16)


def to_blocks(zl, near_code, far_code, near, far, low, high):
    shape = jax.ShapeDtypeStruct((ROWS, high - low), jnp.bfloat16)
    return pl.pallas_call(
        functools.partial(blocks_kernel, low, high),
        out_shape=[shape] * GROUPS,
        in_specs=[smem()] + [vmem()] * 4,
        out_specs=[vmem()] * GROUPS,
        compiler_params=params(),
        name="to_blocks",
    )(zl, near_code, far_code, near, far)


def landed(first, landing):
    rows = lax.broadcasted_iota(jnp.int32, (ROWS, landing.shape[1]), 0) + first
    hits = jnp.where(rows == landing, 1.0, 0.0)
    return jnp.max(hits, axis=1, keepdims=True) > 0.0


def merge_kernel(zl_ref, landing_ref, text_ref, *refs):
    arrived, out_ref = refs[:GROUPS], refs[GROUPS]
    zl = zl_ref[0]
    present = landed(zl * ROWS, landing_ref[...])
    for step in range(GROUPS):
        group = lax.rem(zl - step + GROUPS, GROUPS)
        out_ref[group] = jnp.where(present, arrived[step][...], text_ref[group, :, QW:])


def merge_keys(zl, landing, text, arrived):
    return pl.pallas_call(
        merge_kernel,
        out_shape=jax.ShapeDtypeStruct((GROUPS, ROWS, KW), jnp.bfloat16),
        in_specs=[smem()] + [vmem()] * (2 + GROUPS),
        out_specs=vmem(),
        compiler_params=params(),
        name="merge_keys",
    )(zl, landing, text, *arrived)


def attend_kernel(zl_ref, landing_ref, qdoc_ref, kdoc_ref, text_ref, two_ref, one_ref, own_ref, *refs):
    arrived, out_ref = refs[:GROUPS], refs[GROUPS]
    zl = zl_ref[0]
    present = landed(zl * ROWS, landing_ref[...])
    window = REACH + ROWS
    query_pos = lax.broadcasted_iota(jnp.int32, (ROWS, window), 0) + REACH
    key_pos = lax.broadcasted_iota(jnp.int32, (ROWS, window), 1)
    allowed = (kdoc_ref[...] == qdoc_ref[...]) & (key_pos <= query_pos)
    factor = HD ** (-0.5)
    for step in range(GROUPS):
        group = lax.rem(zl - step + GROUPS, GROUPS)
        queries = jnp.where(present, arrived[step][...], text_ref[group, :, :QW])
        joined = jnp.concatenate([two_ref[group], one_ref[group], own_ref[group]], 0)
        keys, values = joined[:, :HD], joined[:, HD:]
        for head in range(QPG):
            cols = slice(head * HD, (head + 1) * HD)
            scores = lax.dot_general(
                queries[:, cols], keys, (((1,), (1,)), ((), ())), preferred_element_type=jnp.float32
            )
            masked = jnp.where(allowed, scores * factor, -jnp.inf)
            row_max = jnp.max(masked, axis=1, keepdims=True)
            terms = jnp.exp(masked - row_max)
            total = jnp.sum(terms, axis=1, keepdims=True)
            summed = jnp.dot(terms.astype(jnp.bfloat16), values, preferred_element_type=jnp.float32)
            out_ref[group, :, cols] = (summed / total).astype(jnp.bfloat16)


def attend(zl, landing, qdoc, kdoc, text, two, one, own, arrived):
    return pl.pallas_call(
        attend_kernel,
        out_shape=jax.ShapeDtypeStruct((GROUPS, ROWS, QW), jnp.bfloat16),
        in_specs=[smem()] + [vmem()] * (7 + GROUPS),
        out_specs=vmem(),
        compiler_params=params(),
        name="attend",
    )(zl, landing, qdoc, kdoc, text, two, one, own, *arrived)


def after(value, *others):
    return lax.optimization_barrier((value, *others))[0]


def body(text_rows, vision_rows, vision_pos, doc_ids):
    rows = vision_rows.reshape(PER_SOURCE, QW + KW)
    half = lax.axis_index("zh")
    zl = lax.axis_index("zl")
    shard = lax.axis_index(("x", "zh", "y", "c"))

    far_kv_rows = to_other_half(rows[:, QW:])

    marks = doc_ids + 1
    prior_marks = from_behind(marks[SHARD - REACH :], 8)

    pos = vision_pos.reshape(64, PER_SOURCE)
    target = pos // SHARD
    index = jnp.arange(PER_SOURCE, dtype=jnp.int32)

    def slot_code(source):
        own = lax.dynamic_index_in_dim(target, source, 0, keepdims=False)
        same = (own[None, :] == own[:, None]) & (index[:, None] < index[None, :])
        rank = jnp.sum(same.astype(jnp.int32), axis=0)
        column = (own // 16) * 8 + own % 8
        code = jnp.where((own // 8) % 2 == half, column * SLOTS + rank, -1)
        return code.reshape(1, PER_SOURCE)

    hit = target == shard
    skip = jnp.sum((target < shard).astype(jnp.int32), axis=1, keepdims=True)
    rank = jnp.where(hit, index[None, :] - skip, -1)
    slot = jnp.arange(SLOTS, dtype=jnp.int32)
    chosen = rank[:, None, :] == slot[None, :, None]
    local = pos - shard * SHARD + 1
    landing = jnp.sum(jnp.where(chosen, local[:, None, :], 0), axis=2) - 1
    landing = landing.reshape(4, 2, 8 * SLOTS)
    near_code = lax.dynamic_index_in_dim(landing, half, 1, keepdims=False).reshape(1, -1)
    far_code = lax.dynamic_index_in_dim(landing, 1 - half, 1, keepdims=False).reshape(1, -1)
    both = jnp.concatenate([near_code, far_code], 1)

    near_out = to_slots(slot_code(shard), rows)
    near = over_columns(near_out)
    far_slot_code = slot_code(shard ^ 8)

    text = jnp.transpose(text_rows, (1, 0, 2))
    joined_marks = jnp.concatenate([prior_marks, marks], 0)
    kdoc = lax.dynamic_slice_in_dim(joined_marks, zl * ROWS, REACH + ROWS).reshape(1, -1)
    qdoc = lax.dynamic_slice_in_dim(marks, zl * ROWS, ROWS).reshape(-1, 1)
    zl_arr = zl.reshape(1)

    far_q_rows = to_other_half(after(rows[:, :QW], far_kv_rows))

    far_kv = over_columns(to_slots(far_slot_code, far_kv_rows))
    kv_blocks = to_blocks(zl_arr, near_code, far_code, near, far_kv, QW, QW + KW)
    order = (4, 3, 5, 2, 6, 1, 7)
    kv_arrived = [kv_blocks[0]] + [None] * 7
    for step in order:
        kv_arrived[step] = along_head(kv_blocks[step], step)

    far_q = over_columns(to_slots(far_slot_code, far_q_rows))
    own_kv = merge_keys(zl_arr, both, text, kv_arrived)
    one_kv = from_behind(own_kv, 1)

    q_blocks = to_blocks(zl_arr, near_code, far_code, near, far_q, 0, QW)
    q_arrived = [q_blocks[0]] + [None] * 7
    for step in order:
        q_arrived[step] = along_head(q_blocks[step], step)
    two_kv = from_behind(one_kv, 1)

    out = attend(zl_arr, both, qdoc, kdoc, text, two_kv, one_kv, own_kv, q_arrived)
    return jnp.transpose(out, (1, 0, 2))


def solution(mesh):
    fine = Mesh(mesh.devices.reshape(SIZES), AXES)
    in_specs = (
        P(AXES, None, None),
        P(("x", "zh", "y", "c"), "zl", None),
        P(),
        P(("x", "zh", "y", "c")),
    )
    return jax.shard_map(
        body, mesh=fine, in_specs=in_specs, out_specs=P(AXES, None, None), check_vma=False
    )
```

time: 298 us -> 238 us (0.80)
  the two profiles are of different devices: /device:TPU:1 before, /device:TPU:111 now
where the time goes in v1:
time: 238 us; the launch traced here: 237 us
  starting transfers between devices  124 us (52%)
  waiting for transfers between devices  84.4 us (35%)
  Pallas kernels  16.1 us (7%)
  local copies, waits for them, and re-layouts  8.97 us (4%)
  other arithmetic  2.63 us (1%)
    ppermute x14, waiting for transfers between devices, along_head(): lax.ppermute(value, AXES, pairs(lambda x, zh, y, c, zl: (x, zh, y, c, (zl...  61.5 us
    ppermute x14, starting transfers between devices, along_head(): lax.ppermute(value, AXES, pairs(lambda x, zh, y, c, zl: (x, zh, y, c, (zl...  60.6 us
    ppermute x2, starting transfers between devices, to_other_half(): lax.ppermute(value, AXES, pairs(lambda x, zh, y, c, zl: (x, 1 - zh, y, c,...  33.4 us
    all_to_all x3, starting transfers between devices, over_columns(): lax.all_to_all(slots.reshape(32, SLOTS, width), ('x', 'y', 'c'), split_ax...  22.7 us
    ppermute x2, waiting for transfers between devices, to_other_half(): lax.ppermute(value, AXES, pairs(lambda x, zh, y, c, zl: (x, 1 - zh, y, c,...  11.7 us
    pallas_call x1, Pallas kernels, attend(): pl.pallas_call(attend_kernel, out_shape=jax.ShapeDtypeStruct((GROUPS, ROW...  9.68 us
    ppermute x3, starting transfers between devices, from_behind(): lax.ppermute(value, AXES, [(i, i + steps) for i in range(COUNT - steps)])  7.27 us
    all_to_all x3, waiting for transfers between devices, over_columns(): lax.all_to_all(slots.reshape(32, SLOTS, width), ('x', 'y', 'c'), split_ax...  5.78 us
  transfers between devices with their start and end apart: 22, of which 14 were waited for; matrix products, arithmetic and copies ran while one was open for 3% of the time, Pallas kernels for 2%

profile of v1, /device:TPU:111, one launch (start us, length us, event | category | flops | bytes accessed | tf_op | source)
XLA Modules:
  0.0 236.5 jit_solution(724061030853968476)
XLA Ops:
  1.0 12.7 %collective-permute-start.1 = (bf16[512,256]{1,0:T(8,128)(2,1)S(1)}, bf16[512,256]{1,0:T(8,128)(2,1)S(1)}, u32[]{:S(2)}, u32[]{:S(2)}) collective-permute-start(bf16[512,256]{1,0:T(8,128)(2,1)S(1)} %slice.12), channel_id=1, source_target_pairs={{0,64},{1,65},{2,66},{3,67},{4,68},{5,69},{6,70},{7,71},{8,72},{9,... | collective-permute-start | bytes 786440 | tf_op jit(solution)/shard_map/ppermute | solution.py:43
  15.2 11.7 %collective-permute-done.1.rows_ref = bf16[512,256]{1,0:T(8,128)(2,1)S(1)} collective-permute-done((bf16[512,256]{1,0:T(8,128)(2,1)S(1)}, bf16[512,256]{1,0:T(8,128)(2,1)S(1)}, u32[]{:S(2)}, u32[]{:S(2)}) %collective-permute-start.1) | collective-permute-done | bytes 262176 | tf_op jit(solution)/shard_map/ppermute | solution.py:43
  27.9 8.7 %all-to-all-start.1 = ((bf16[32,16,256]{2,1,0:T(8,128)(2,1)}), bf16[32,16,256]{2,1,0:T(8,128)(2,1)S(1)}, u32[]{:S(2)}, u32[]{:S(2)}) async-start(bf16[32,16,256]{2,1,0:T(8,128)(2,1)} %bitcast.12), calls=%async_computation.1 | async-start | bytes 524288 | tf_op jit(solution)/shard_map/all_to_all | solution.py:56
  38.3 4.6 %all-to-all-done.1 = bf16[32,16,256]{2,1,0:T(8,128)(2,1)S(1)} async-done(((bf16[32,16,256]{2,1,0:T(8,128)(2,1)}), bf16[32,16,256]{2,1,0:T(8,128)(2,1)S(1)}, u32[]{:S(2)}, u32[]{:S(2)}) %all-to-all-start.1) | async-done | bytes 262176 | tf_op jit(solution)/shard_map/all_to_all | solution.py:56
  42.9 6.5 %all-to-all-start = ((bf16[32,16,768]{2,1,0:T(8,128)(2,1)}), bf16[32,16,768]{2,1,0:T(8,128)(2,1)S(1)}, u32[]{:S(2)}, u32[]{:S(2)}) async-start(bf16[32,16,768]{2,1,0:T(8,128)(2,1)} %bitcast.8), calls=%async_computation | async-start | bytes 1572864 | tf_op jit(solution)/shard_map/all_to_all | solution.py:56
  51.6 20.7 %collective-permute-start.11 = (bf16[512,512]{1,0:T(8,128)(2,1)}, bf16[512,512]{1,0:T(8,128)(2,1)S(1)}, u32[]{:S(2)}, u32[]{:S(2)}) collective-permute-start(bf16[512,512]{1,0:T(8,128)(2,1)} %slice.13), channel_id=1, source_target_pairs={{0,64},{1,65},{2,66},{3,67},{4,68},{5,69},{6,70},{7,71},{8,72},{9,... | collective-permute-start | bytes 1572872 | tf_op jit(solution)/shard_map/ppermute | solution.py:43
  75.0 4.7 %collective-permute-start.3 = (bf16[128,256]{1,0:T(8,128)(2,1)S(1)}, bf16[128,256]{1,0:T(8,128)(2,1)S(1)}, u32[]{:S(2)}, u32[]{:S(2)}) collective-permute-start(bf16[128,256]{1,0:T(8,128)(2,1)S(1)} %get-tuple-element.24), channel_id=1, source_target_pairs={{0,2},{1,3},{2,4},{3,5},{4,6},{5,7},{6,0},{7,1},{8,10},{9,11},{10,... | collective-permute-start | bytes 196616 | tf_op jit(solution)/shard_map/ppermute | solution.py:47
  79.7 6.5 %collective-permute-start.4 = (bf16[128,256]{1,0:T(8,128)(2,1)S(1)}, bf16[128,256]{1,0:T(8,128)(2,1)S(1)}, u32[]{:S(2)}, u32[]{:S(2)}) collective-permute-start(bf16[128,256]{1,0:T(8,128)(2,1)S(1)} %get-tuple-element.25), channel_id=1, source_target_pairs={{0,3},{1,4},{2,5},{3,6},{4,7},{5,0},{6,1},{7,2},{8,11},{9,12},{10,... | collective-permute-start | bytes 196616 | tf_op jit(solution)/shard_map/ppermute | solution.py:47
  89.9 7.4 %collective-permute-done.2.refs_1_ = bf16[128,256]{1,0:T(8,128)(2,1)S(1)} collective-permute-done((bf16[128,256]{1,0:T(8,128)(2,1)S(1)}, bf16[128,256]{1,0:T(8,128)(2,1)S(1)}, u32[]{:S(2)}, u32[]{:S(2)}) %collective-permute-start.2) | collective-permute-done | bytes 65568 | tf_op jit(solution)/shard_map/ppermute | solution.py:47
  99.2 14.2 %collective-permute-done.3.refs_2_ = bf16[128,256]{1,0:T(8,128)(2,1)S(1)} collective-permute-done((bf16[128,256]{1,0:T(8,128)(2,1)S(1)}, bf16[128,256]{1,0:T(8,128)(2,1)S(1)}, u32[]{:S(2)}, u32[]{:S(2)}) %collective-permute-start.3) | collective-permute-done | bytes 65568 | tf_op jit(solution)/shard_map/ppermute | solution.py:47
  115.7 4.8 %collective-permute-start.8 = (bf16[128,256]{1,0:T(8,128)(2,1)S(1)}, bf16[128,256]{1,0:T(8,128)(2,1)S(1)}, u32[]{:S(2)}, u32[]{:S(2)}) collective-permute-start(bf16[128,256]{1,0:T(8,128)(2,1)S(1)} %get-tuple-element.29), channel_id=1, source_target_pairs={{0,7},{1,0},{2,1},{3,2},{4,3},{5,4},{6,5},{7,6},{8,15},{9,8},{10,9... | collective-permute-start | bytes 196616 | tf_op jit(solution)/shard_map/ppermute | solution.py:47
  120.5 4.4 %collective-permute-done.5.refs_4_ = bf16[128,256]{1,0:T(8,128)(2,1)S(1)} collective-permute-done((bf16[128,256]{1,0:T(8,128)(2,1)S(1)}, bf16[128,256]{1,0:T(8,128)(2,1)S(1)}, u32[]{:S(2)}, u32[]{:S(2)}) %collective-permute-start.5) | collective-permute-done | bytes 65568 | tf_op jit(solution)/shard_map/ppermute | solution.py:47
  127.7 4.9 %collective-permute-done.7.refs_6_ = bf16[128,256]{1,0:T(8,128)(2,1)S(1)} collective-permute-done((bf16[128,256]{1,0:T(8,128)(2,1)S(1)}, bf16[128,256]{1,0:T(8,128)(2,1)S(1)}, u32[]{:S(2)}, u32[]{:S(2)}) %collective-permute-start.7) | collective-permute-done | bytes 65568 | tf_op jit(solution)/shard_map/ppermute | solution.py:47
  132.6 3.7 %collective-permute-done.8.refs_7_ = bf16[128,256]{1,0:T(8,128)(2,1)S(1)} collective-permute-done((bf16[128,256]{1,0:T(8,128)(2,1)S(1)}, bf16[128,256]{1,0:T(8,128)(2,1)S(1)}, u32[]{:S(2)}, u32[]{:S(2)}) %collective-permute-start.8) | collective-permute-done | bytes 65568 | tf_op jit(solution)/shard_map/ppermute | solution.py:47
  139.6 7.5 %all-to-all-start.2 = ((bf16[32,16,512]{2,1,0:T(8,128)(2,1)}), bf16[32,16,512]{2,1,0:T(8,128)(2,1)S(1)}, u32[]{:S(2)}, u32[]{:S(2)}) async-start(bf16[32,16,512]{2,1,0:T(8,128)(2,1)} %bitcast.14), calls=%async_computation.2 | async-start | bytes 1048576 | tf_op jit(solution)/shard_map/all_to_all | solution.py:56
  147.1 4.3 %collective-permute-done.9.one_ref = bf16[8,128,256]{2,1,0:T(8,128)(2,1)} collective-permute-done((bf16[8,128,256]{2,1,0:T(8,128)(2,1)S(1)}, bf16[8,128,256]{2,1,0:T(8,128)(2,1)}, u32[]{:S(2)}, u32[]{:S(2)}) %collective-permute-start.9) | collective-permute-done | bytes 524320 | tf_op jit(solution)/shard_map/ppermute | solution.py:51
  162.4 8.9 %collective-permute-start.13 = (bf16[128,512]{1,0:T(8,128)(2,1)}, bf16[128,512]{1,0:T(8,128)(2,1)S(1)}, u32[]{:S(2)}, u32[]{:S(2)}) collective-permute-start(bf16[128,512]{1,0:T(8,128)(2,1)} %get-tuple-element.33), channel_id=1, source_target_pairs={{0,2},{1,3},{2,4},{3,5},{4,6},{5,7},{6,0},{7,1},{8,10},{9,11},{10,... | collective-permute-start | bytes 393224 | tf_op jit(solution)/shard_map/ppermute | solution.py:47
  171.3 9.0 %collective-permute-start.14 = (bf16[128,512]{1,0:T(8,128)(2,1)}, bf16[128,512]{1,0:T(8,128)(2,1)S(1)}, u32[]{:S(2)}, u32[]{:S(2)}) collective-permute-start(bf16[128,512]{1,0:T(8,128)(2,1)} %get-tuple-element.34), channel_id=1, source_target_pairs={{0,3},{1,4},{2,5},{3,6},{4,7},{5,0},{6,1},{7,2},{8,11},{9,12},{10,... | collective-permute-start | bytes 393224 | tf_op jit(solution)/shard_map/ppermute | solution.py:47
  186.0 5.3 %collective-permute-start.16 = (bf16[128,512]{1,0:T(8,128)(2,1)}, bf16[128,512]{1,0:T(8,128)(2,1)S(1)}, u32[]{:S(2)}, u32[]{:S(2)}) collective-permute-start(bf16[128,512]{1,0:T(8,128)(2,1)} %copy-done.3), channel_id=1, source_target_pairs={{0,5},{1,6},{2,7},{3,0},{4,1},{5,2},{6,3},{7,4},{8,13},{9,14},{10,... | collective-permute-start | bytes 393224 | tf_op jit(solution)/shard_map/ppermute | solution.py:47
  191.3 6.7 %collective-permute-start.17 = (bf16[128,512]{1,0:T(8,128)(2,1)}, bf16[128,512]{1,0:T(8,128)(2,1)S(1)}, u32[]{:S(2)}, u32[]{:S(2)}) collective-permute-start(bf16[128,512]{1,0:T(8,128)(2,1)} %copy-done.2), channel_id=1, source_target_pairs={{0,6},{1,7},{2,0},{3,1},{4,2},{5,3},{6,4},{7,5},{8,14},{9,15},{10,... | collective-permute-start | bytes 393224 | tf_op jit(solution)/shard_map/ppermute | solution.py:47
  201.1 15.2 %collective-permute-done.15.refs_4_ = bf16[128,512]{1,0:T(8,128)(2,1)S(1)} collective-permute-done((bf16[128,512]{1,0:T(8,128)(2,1)}, bf16[128,512]{1,0:T(8,128)(2,1)S(1)}, u32[]{:S(2)}, u32[]{:S(2)}) %collective-permute-start.15) | collective-permute-done | bytes 131104 | tf_op jit(solution)/shard_map/ppermute | solution.py:47
  216.3 3.5 %collective-permute-done.17.refs_6_ = bf16[128,512]{1,0:T(8,128)(2,1)S(1)} collective-permute-done((bf16[128,512]{1,0:T(8,128)(2,1)}, bf16[128,512]{1,0:T(8,128)(2,1)S(1)}, u32[]{:S(2)}, u32[]{:S(2)}) %collective-permute-start.17) | collective-permute-done | bytes 131104 | tf_op jit(solution)/shard_map/ppermute | solution.py:47
  219.7 5.5 %collective-permute-done.18.refs_7_ = bf16[128,512]{1,0:T(8,128)(2,1)S(1)} collective-permute-done((bf16[128,512]{1,0:T(8,128)(2,1)}, bf16[128,512]{1,0:T(8,128)(2,1)S(1)}, u32[]{:S(2)}, u32[]{:S(2)}) %collective-permute-start.18) | collective-permute-done | bytes 131104 | tf_op jit(solution)/shard_map/ppermute | solution.py:47
  225.3 9.7 %attend.1 = bf16[8,128,512]{2,1,0:T(8,128)(2,1)S(1)} custom-call(s32[1]{0:T(128)} %bitcast.zl_ref, s32[1,1024]{1,0:T(1,128)S(1)} %pad_add_fusion.landing_ref, s32[128,1]{1,0:T(8,128)S(1)} %copy.12.qdoc_ref, s32[1,384]{1,0:T(1,128)S(1)} %reshape.111.kdoc_ref, bf16[8,128,768]{2,1,0:T(8,128)(2,1)S(1)} %bitcast.23, ...), custom_call_target="tpu_custom_call" | custom-call | tf_op jit(solution)/shard_map/attend/pallas_call | solution.py:178
  (60 shorter events, 45.1 us)
Async XLA Ops:
  0.0 36.8 %copy-start = (bf16[512,1,768]{2,0,1:T(8,128)(2,1)S(1)}, bf16[512,1,768]{2,0,1:T(8,128)(2,1)}, u32[]{:S(2)}) copy-start(bf16[512,1,768]{2,0,1:T(8,128)(2,1)} %param.5) | copy-start | bytes 2359300
  1.0 25.8 %collective-permute-start.1 = (bf16[512,256]{1,0:T(8,128)(2,1)S(1)}, bf16[512,256]{1,0:T(8,128)(2,1)S(1)}, u32[]{:S(2)}, u32[]{:S(2)}) collective-permute-start(bf16[512,256]{1,0:T(8,128)(2,1)S(1)} %slice.12), channel_id=1, source_target_pairs={{0,64},{1,65},{2,66},{3,67},{4,68},{5,69},{6,70},{7,71},{8,72},{9,... | collective-permute-start | bytes 786440 | tf_op jit(solution)/shard_map/ppermute | solution.py:43
  27.9 15.0 %all-to-all-start.1 = ((bf16[32,16,256]{2,1,0:T(8,128)(2,1)}), bf16[32,16,256]{2,1,0:T(8,128)(2,1)S(1)}, u32[]{:S(2)}, u32[]{:S(2)}) async-start(bf16[32,16,256]{2,1,0:T(8,128)(2,1)} %bitcast.12), calls=%async_computation.1 | async-start | bytes 524288 | tf_op jit(solution)/shard_map/all_to_all | solution.py:56
  42.9 29.4 %all-to-all-start = ((bf16[32,16,768]{2,1,0:T(8,128)(2,1)}), bf16[32,16,768]{2,1,0:T(8,128)(2,1)S(1)}, u32[]{:S(2)}, u32[]{:S(2)}) async-start(bf16[32,16,768]{2,1,0:T(8,128)(2,1)} %bitcast.8), calls=%async_computation | async-start | bytes 1572864 | tf_op jit(solution)/shard_map/all_to_all | solution.py:56
  51.6 86.8 %collective-permute-start.11 = (bf16[512,512]{1,0:T(8,128)(2,1)}, bf16[512,512]{1,0:T(8,128)(2,1)S(1)}, u32[]{:S(2)}, u32[]{:S(2)}) collective-permute-start(bf16[512,512]{1,0:T(8,128)(2,1)} %slice.13), channel_id=1, source_target_pairs={{0,64},{1,65},{2,66},{3,67},{4,68},{5,69},{6,70},{7,71},{8,72},{9,... | collective-permute-start | bytes 1572872 | tf_op jit(solution)/shard_map/ppermute | solution.py:43
  73.1 24.2 %collective-permute-start.2 = (bf16[128,256]{1,0:T(8,128)(2,1)S(1)}, bf16[128,256]{1,0:T(8,128)(2,1)S(1)}, u32[]{:S(2)}, u32[]{:S(2)}) collective-permute-start(bf16[128,256]{1,0:T(8,128)(2,1)S(1)} %get-tuple-element.23), channel_id=1, source_target_pairs={{0,1},{1,2},{2,3},{3,4},{4,5},{5,6},{6,7},{7,0},{8,9},{9,10},{10,1... | collective-permute-start | bytes 196616 | tf_op jit(solution)/shard_map/ppermute | solution.py:47
  75.0 38.3 %collective-permute-start.3 = (bf16[128,256]{1,0:T(8,128)(2,1)S(1)}, bf16[128,256]{1,0:T(8,128)(2,1)S(1)}, u32[]{:S(2)}, u32[]{:S(2)}) collective-permute-start(bf16[128,256]{1,0:T(8,128)(2,1)S(1)} %get-tuple-element.24), channel_id=1, source_target_pairs={{0,2},{1,3},{2,4},{3,5},{4,6},{5,7},{6,0},{7,1},{8,10},{9,11},{10,... | collective-permute-start | bytes 196616 | tf_op jit(solution)/shard_map/ppermute | solution.py:47
  79.7 36.0 %collective-permute-start.4 = (bf16[128,256]{1,0:T(8,128)(2,1)S(1)}, bf16[128,256]{1,0:T(8,128)(2,1)S(1)}, u32[]{:S(2)}, u32[]{:S(2)}) collective-permute-start(bf16[128,256]{1,0:T(8,128)(2,1)S(1)} %get-tuple-element.25), channel_id=1, source_target_pairs={{0,3},{1,4},{2,5},{3,6},{4,7},{5,0},{6,1},{7,2},{8,11},{9,12},{10,... | collective-permute-start | bytes 196616 | tf_op jit(solution)/shard_map/ppermute | solution.py:47
  88.0 37.0 %collective-permute-start.5 = (bf16[128,256]{1,0:T(8,128)(2,1)S(1)}, bf16[128,256]{1,0:T(8,128)(2,1)S(1)}, u32[]{:S(2)}, u32[]{:S(2)}) collective-permute-start(bf16[128,256]{1,0:T(8,128)(2,1)S(1)} %get-tuple-element.26), channel_id=1, source_target_pairs={{0,4},{1,5},{2,6},{3,7},{4,0},{5,1},{6,2},{7,3},{8,12},{9,13},{10,... | collective-permute-start | bytes 196616 | tf_op jit(solution)/shard_map/ppermute | solution.py:47
  97.2 30.5 %collective-permute-start.6 = (bf16[128,256]{1,0:T(8,128)(2,1)S(1)}, bf16[128,256]{1,0:T(8,128)(2,1)S(1)}, u32[]{:S(2)}, u32[]{:S(2)}) collective-permute-start(bf16[128,256]{1,0:T(8,128)(2,1)S(1)} %get-tuple-element.27), channel_id=1, source_target_pairs={{0,5},{1,6},{2,7},{3,0},{4,1},{5,2},{6,3},{7,4},{8,13},{9,14},{10,... | collective-permute-start | bytes 196616 | tf_op jit(solution)/shard_map/ppermute | solution.py:47
  113.3 19.2 %collective-permute-start.7 = (bf16[128,256]{1,0:T(8,128)(2,1)S(1)}, bf16[128,256]{1,0:T(8,128)(2,1)S(1)}, u32[]{:S(2)}, u32[]{:S(2)}) collective-permute-start(bf16[128,256]{1,0:T(8,128)(2,1)S(1)} %get-tuple-element.28), channel_id=1, source_target_pairs={{0,6},{1,7},{2,0},{3,1},{4,2},{5,3},{6,4},{7,5},{8,14},{9,15},{10,... | collective-permute-start | bytes 196616 | tf_op jit(solution)/shard_map/ppermute | solution.py:47
  115.7 20.6 %collective-permute-start.8 = (bf16[128,256]{1,0:T(8,128)(2,1)S(1)}, bf16[128,256]{1,0:T(8,128)(2,1)S(1)}, u32[]{:S(2)}, u32[]{:S(2)}) collective-permute-start(bf16[128,256]{1,0:T(8,128)(2,1)S(1)} %get-tuple-element.29), channel_id=1, source_target_pairs={{0,7},{1,0},{2,1},{3,2},{4,3},{5,4},{6,5},{7,6},{8,15},{9,8},{10,9... | collective-permute-start | bytes 196616 | tf_op jit(solution)/shard_map/ppermute | solution.py:47
  136.4 15.0 %collective-permute-start.9 = (bf16[8,128,256]{2,1,0:T(8,128)(2,1)S(1)}, bf16[8,128,256]{2,1,0:T(8,128)(2,1)}, u32[]{:S(2)}, u32[]{:S(2)}) collective-permute-start(bf16[8,128,256]{2,1,0:T(8,128)(2,1)S(1)} %merge_keys.1.own_ref), channel_id=1, source_target_pairs={{0,1},{1,2},{2,3},{3,4},{4,5},{5,6},{6,7},{7,8},{8,9},{9,10},{10,1... | collective-permute-start | bytes 1572872 | tf_op jit(solution)/shard_map/ppermute | solution.py:51
  139.6 16.4 %all-to-all-start.2 = ((bf16[32,16,512]{2,1,0:T(8,128)(2,1)}), bf16[32,16,512]{2,1,0:T(8,128)(2,1)S(1)}, u32[]{:S(2)}, u32[]{:S(2)}) async-start(bf16[32,16,512]{2,1,0:T(8,128)(2,1)} %bitcast.14), calls=%async_computation.2 | async-start | bytes 1048576 | tf_op jit(solution)/shard_map/all_to_all | solution.py:56
  151.4 73.9 %collective-permute-start.10 = (bf16[8,128,256]{2,1,0:T(8,128)(2,1)}, bf16[8,128,256]{2,1,0:T(8,128)(2,1)}, u32[]{:S(2)}, u32[]{:S(2)}) collective-permute-start(bf16[8,128,256]{2,1,0:T(8,128)(2,1)} %collective-permute-done.9.one_ref), channel_id=1, source_target_pairs={{0,1},{1,2},{2,3},{3,4},{4,5},{5,6},{6,7},{7,8},{8,9},{9,10},{10,1... | collective-permute-start | bytes 1572872 | tf_op jit(solution)/shard_map/ppermute | solution.py:51
  159.2 0.7 copy-start.3
  160.5 25.5 %collective-permute-start.12 = (bf16[128,512]{1,0:T(8,128)(2,1)}, bf16[128,512]{1,0:T(8,128)(2,1)S(1)}, u32[]{:S(2)}, u32[]{:S(2)}) collective-permute-start(bf16[128,512]{1,0:T(8,128)(2,1)} %get-tuple-element.32), channel_id=1, source_target_pairs={{0,1},{1,2},{2,3},{3,4},{4,5},{5,6},{6,7},{7,0},{8,9},{9,10},{10,1... | collective-permute-start | bytes 393224 | tf_op jit(solution)/shard_map/ppermute | solution.py:47
  162.4 28.9 %collective-permute-start.13 = (bf16[128,512]{1,0:T(8,128)(2,1)}, bf16[128,512]{1,0:T(8,128)(2,1)S(1)}, u32[]{:S(2)}, u32[]{:S(2)}) collective-permute-start(bf16[128,512]{1,0:T(8,128)(2,1)} %get-tuple-element.33), channel_id=1, source_target_pairs={{0,2},{1,3},{2,4},{3,5},{4,6},{5,7},{6,0},{7,1},{8,10},{9,11},{10,... | collective-permute-start | bytes 393224 | tf_op jit(solution)/shard_map/ppermute | solution.py:47
  171.3 26.7 %collective-permute-start.14 = (bf16[128,512]{1,0:T(8,128)(2,1)}, bf16[128,512]{1,0:T(8,128)(2,1)S(1)}, u32[]{:S(2)}, u32[]{:S(2)}) collective-permute-start(bf16[128,512]{1,0:T(8,128)(2,1)} %get-tuple-element.34), channel_id=1, source_target_pairs={{0,3},{1,4},{2,5},{3,6},{4,7},{5,0},{6,1},{7,2},{8,11},{9,12},{10,... | collective-permute-start | bytes 393224 | tf_op jit(solution)/shard_map/ppermute | solution.py:47
  181.0 3.0 %collective-permute-start = (s32[256]{0:T(256)S(1)}, s32[256]{0:T(256)S(1)}, u32[]{:S(2)}, u32[]{:S(2)}) collective-permute-start(s32[256]{0:T(256)S(1)} %slice.9), channel_id=1, source_target_pairs={{0,8},{1,9},{2,10},{3,11},{4,12},{5,13},{6,14},{7,15},{8,16},{9,17... | collective-permute-start | bytes 3080 | tf_op jit(solution)/shard_map/ppermute | solution.py:51
  184.0 32.2 %collective-permute-start.15 = (bf16[128,512]{1,0:T(8,128)(2,1)}, bf16[128,512]{1,0:T(8,128)(2,1)S(1)}, u32[]{:S(2)}, u32[]{:S(2)}) collective-permute-start(bf16[128,512]{1,0:T(8,128)(2,1)} %copy-done.4), channel_id=1, source_target_pairs={{0,4},{1,5},{2,6},{3,7},{4,0},{5,1},{6,2},{7,3},{8,12},{9,13},{10,... | collective-permute-start | bytes 393224 | tf_op jit(solution)/shard_map/ppermute | solution.py:47
  186.0 30.3 %collective-permute-start.16 = (bf16[128,512]{1,0:T(8,128)(2,1)}, bf16[128,512]{1,0:T(8,128)(2,1)S(1)}, u32[]{:S(2)}, u32[]{:S(2)}) collective-permute-start(bf16[128,512]{1,0:T(8,128)(2,1)} %copy-done.3), channel_id=1, source_target_pairs={{0,5},{1,6},{2,7},{3,0},{4,1},{5,2},{6,3},{7,4},{8,13},{9,14},{10,... | collective-permute-start | bytes 393224 | tf_op jit(solution)/shard_map/ppermute | solution.py:47
  191.3 28.5 %collective-permute-start.17 = (bf16[128,512]{1,0:T(8,128)(2,1)}, bf16[128,512]{1,0:T(8,128)(2,1)S(1)}, u32[]{:S(2)}, u32[]{:S(2)}) collective-permute-start(bf16[128,512]{1,0:T(8,128)(2,1)} %copy-done.2), channel_id=1, source_target_pairs={{0,6},{1,7},{2,0},{3,1},{4,2},{5,3},{6,4},{7,5},{8,14},{9,15},{10,... | collective-permute-start | bytes 393224 | tf_op jit(solution)/shard_map/ppermute | solution.py:47
  198.0 27.3 %collective-permute-start.18 = (bf16[128,512]{1,0:T(8,128)(2,1)}, bf16[128,512]{1,0:T(8,128)(2,1)S(1)}, u32[]{:S(2)}, u32[]{:S(2)}) collective-permute-start(bf16[128,512]{1,0:T(8,128)(2,1)} %copy-done.1), channel_id=1, source_target_pairs={{0,7},{1,0},{2,1},{3,2},{4,3},{5,4},{6,5},{7,6},{8,15},{9,8},{10,9... | collective-permute-start | bytes 393224 | tf_op jit(solution)/shard_map/ppermute | solution.py:47
  (3 other events, 1.9 us)

commit v2 on v1

--- a/solution.py
+++ b/solution.py
@@ -147,8 +147,8 @@
     )(zl, landing, text, *arrived)
 
 
-def attend_kernel(zl_ref, landing_ref, qdoc_ref, kdoc_ref, text_ref, two_ref, one_ref, own_ref, *refs):
-    arrived, out_ref = refs[:GROUPS], refs[GROUPS]
+def attend_kernel(steps, first_steps, zl_ref, landing_ref, qdoc_ref, kdoc_ref, text_ref, two_ref, one_ref, own_ref, *refs):
+    arrived, earlier, out_ref = refs[: len(steps)], refs[len(steps) : -1], refs[-1]
     zl = zl_ref[0]
     present = landed(zl * ROWS, landing_ref[...])
     window = REACH + ROWS
@@ -156,11 +156,14 @@
     key_pos = lax.broadcasted_iota(jnp.int32, (ROWS, window), 1)
     allowed = (kdoc_ref[...] == qdoc_ref[...]) & (key_pos <= query_pos)
     factor = HD ** (-0.5)
-    for step in range(GROUPS):
+    for place, step in enumerate(first_steps):
+        out_ref[lax.rem(zl - step + GROUPS, GROUPS)] = earlier[0][place]
+    for place, step in enumerate(steps):
         group = lax.rem(zl - step + GROUPS, GROUPS)
-        queries = jnp.where(present, arrived[step][...], text_ref[group, :, :QW])
+        queries = jnp.where(present, arrived[place][...], text_ref[group, :, :QW])
         joined = jnp.concatenate([two_ref[group], one_ref[group], own_ref[group]], 0)
         keys, values = joined[:, :HD], joined[:, HD:]
+        row = group if first_steps else place
         for head in range(QPG):
             cols = slice(head * HD, (head + 1) * HD)
             scores = lax.dot_general(
@@ -171,22 +174,19 @@
             terms = jnp.exp(masked - row_max)
             total = jnp.sum(terms, axis=1, keepdims=True)
             summed = jnp.dot(terms.astype(jnp.bfloat16), values, preferred_element_type=jnp.float32)
-            out_ref[group, :, cols] = (summed / total).astype(jnp.bfloat16)
-
-
-def attend(zl, landing, qdoc, kdoc, text, two, one, own, arrived):
-    return pl.pallas_call(
-        attend_kernel,
-        out_shape=jax.ShapeDtypeStruct((GROUPS, ROWS, QW), jnp.bfloat16),
-        in_specs=[smem()] + [vmem()] * (7 + GROUPS),
+            out_ref[row, :, cols] = (summed / total).astype(jnp.bfloat16)
+
+
+def attend(steps, first_steps, common, arrived, earlier):
+    count = GROUPS if first_steps else len(steps)
+    return pl.pallas_call(
+        functools.partial(attend_kernel, steps, first_steps),
+        out_shape=jax.ShapeDtypeStruct((count, ROWS, QW), jnp.bfloat16),
+        in_specs=[smem()] + [vmem()] * (7 + len(steps) + len(earlier)),
         out_specs=vmem(),
         compiler_params=params(),
         name="attend",
-    )(zl, landing, qdoc, kdoc, text, two, one, own, *arrived)
-
-
-def after(value, *others):
-    return lax.optimization_barrier((value, *others))[0]
+    )(*common, *[arrived[step] for step in steps], *earlier)
 
 
 def body(text_rows, vision_rows, vision_pos, doc_ids):
@@ -196,6 +196,7 @@
     shard = lax.axis_index(("x", "zh", "y", "c"))
 
     far_kv_rows = to_other_half(rows[:, QW:])
+    far_q_rows = to_other_half(rows[:, :QW])
 
     marks = doc_ids + 1
     prior_marks = from_behind(marks[SHARD - REACH :], 8)
@@ -234,8 +235,6 @@
     qdoc = lax.dynamic_slice_in_dim(marks, zl * ROWS, ROWS).reshape(-1, 1)
     zl_arr = zl.reshape(1)
 
-    far_q_rows = to_other_half(after(rows[:, :QW], far_kv_rows))
-
     far_kv = over_columns(to_slots(far_slot_code, far_kv_rows))
     kv_blocks = to_blocks(zl_arr, near_code, far_code, near, far_kv, QW, QW + KW)
     order = (4, 3, 5, 2, 6, 1, 7)
@@ -253,7 +252,10 @@
         q_arrived[step] = along_head(q_blocks[step], step)
     two_kv = from_behind(one_kv, 1)
 
-    out = attend(zl_arr, both, qdoc, kdoc, text, two_kv, one_kv, own_kv, q_arrived)
+    common = (zl_arr, both, qdoc, kdoc, text, two_kv, one_kv, own_kv)
+    first_steps, last_steps = (0, 4, 3, 5), (2, 6, 1, 7)
+    first = attend(first_steps, (), common, q_arrived, ())
+    out = attend(last_steps, first_steps, common, q_arrived, (first,))
     return jnp.transpose(out, (1, 0, 2))
 
 

time: 238 us -> 240 us (level)
  the two profiles are of different devices: /device:TPU:111 before, /device:TPU:1 now
where the time goes in v2:
time: 240 us; the launch traced here: 238 us
  starting transfers between devices  142 us (59%)
  waiting for transfers between devices  67.5 us (28%)
  Pallas kernels  16.8 us (7%)
  local copies, waits for them, and re-layouts  9.77 us (4%)
    ppermute x14, starting transfers between devices, along_head(): lax.ppermute(value, AXES, pairs(lambda x, zh, y, c, zl: (x, zh, y, c, (zl...  82.6 us
    ppermute x14, waiting for transfers between devices, along_head(): lax.ppermute(value, AXES, pairs(lambda x, zh, y, c, zl: (x, zh, y, c, (zl...  42 us
    ppermute x2, starting transfers between devices, to_other_half(): lax.ppermute(value, AXES, pairs(lambda x, zh, y, c, zl: (x, 1 - zh, y, c,...  28.3 us
    all_to_all x3, starting transfers between devices, over_columns(): lax.all_to_all(slots.reshape(32, SLOTS, width), ('x', 'y', 'c'), split_ax...  23.5 us
    all_to_all x3, waiting for transfers between devices, over_columns(): lax.all_to_all(slots.reshape(32, SLOTS, width), ('x', 'y', 'c'), split_ax...  12.3 us
    pallas_call x2, Pallas kernels, attend(): pl.pallas_call(functools.partial(attend_kernel, steps, first_steps), out_...  11.2 us
    ppermute x3, waiting for transfers between devices, from_behind(): lax.ppermute(value, AXES, [(i, i + steps) for i in range(COUNT - steps)])  9.29 us
    ppermute x3, starting transfers between devices, from_behind(): lax.ppermute(value, AXES, [(i, i + steps) for i in range(COUNT - steps)])  7.42 us
  transfers between devices with their start and end apart: 22, of which 10 were waited for; matrix products, arithmetic and copies ran while one was open for 2% of the time, Pallas kernels for 4%

profile of v2, /device:TPU:1, one launch (start us, length us, event | category | flops | bytes accessed | tf_op | source)
XLA Modules:
  0.0 238.4 jit_solution(8447572108752054726)
XLA Ops:
  1.0 16.3 %collective-permute-start.1 = (bf16[512,256]{1,0:T(8,128)(2,1)S(1)}, bf16[512,256]{1,0:T(8,128)(2,1)S(1)}, u32[]{:S(2)}, u32[]{:S(2)}) collective-permute-start(bf16[512,256]{1,0:T(8,128)(2,1)S(1)} %slice.12), channel_id=1, source_target_pairs={{0,64},{1,65},{2,66},{3,67},{4,68},{5,69},{6,70},{7,71},{8,72},{9,... | collective-permute-start | bytes 786440 | tf_op jit(solution)/shard_map/ppermute | solution.py:43
  18.7 3.9 %collective-permute-done.1.rows_ref = bf16[512,256]{1,0:T(8,128)(2,1)S(1)} collective-permute-done((bf16[512,256]{1,0:T(8,128)(2,1)S(1)}, bf16[512,256]{1,0:T(8,128)(2,1)S(1)}, u32[]{:S(2)}, u32[]{:S(2)}) %collective-permute-start.1) | collective-permute-done | bytes 262176 | tf_op jit(solution)/shard_map/ppermute | solution.py:43
  23.6 9.4 %all-to-all-start.1 = ((bf16[32,16,256]{2,1,0:T(8,128)(2,1)}), bf16[32,16,256]{2,1,0:T(8,128)(2,1)S(1)}, u32[]{:S(2)}, u32[]{:S(2)}) async-start(bf16[32,16,256]{2,1,0:T(8,128)(2,1)} %bitcast.12), calls=%async_computation.1 | async-start | bytes 524288 | tf_op jit(solution)/shard_map/all_to_all | solution.py:56
  34.7 7.3 %all-to-all-done.1 = bf16[32,16,256]{2,1,0:T(8,128)(2,1)S(1)} async-done(((bf16[32,16,256]{2,1,0:T(8,128)(2,1)}), bf16[32,16,256]{2,1,0:T(8,128)(2,1)S(1)}, u32[]{:S(2)}, u32[]{:S(2)}) %all-to-all-start.1) | async-done | bytes 262176 | tf_op jit(solution)/shard_map/all_to_all | solution.py:56
  42.0 3.8 %all-to-all-start = ((bf16[32,16,768]{2,1,0:T(8,128)(2,1)}), bf16[32,16,768]{2,1,0:T(8,128)(2,1)S(1)}, u32[]{:S(2)}, u32[]{:S(2)}) async-start(bf16[32,16,768]{2,1,0:T(8,128)(2,1)} %bitcast.8), calls=%async_computation | async-start | bytes 1572864 | tf_op jit(solution)/shard_map/all_to_all | solution.py:56
  46.6 12.0 %collective-permute-start.11 = (bf16[512,512]{1,0:T(8,128)(2,1)}, bf16[512,512]{1,0:T(8,128)(2,1)S(1)}, u32[]{:S(2)}, u32[]{:S(2)}) collective-permute-start(bf16[512,512]{1,0:T(8,128)(2,1)} %slice.13), channel_id=1, source_target_pairs={{0,64},{1,65},{2,66},{3,67},{4,68},{5,69},{6,70},{7,71},{8,72},{9,... | collective-permute-start | bytes 1572872 | tf_op jit(solution)/shard_map/ppermute | solution.py:43
  60.8 19.4 %collective-permute-start.2 = (bf16[128,256]{1,0:T(8,128)(2,1)S(1)}, bf16[128,256]{1,0:T(8,128)(2,1)S(1)}, u32[]{:S(2)}, u32[]{:S(2)}) collective-permute-start(bf16[128,256]{1,0:T(8,128)(2,1)S(1)} %get-tuple-element.22), channel_id=1, source_target_pairs={{0,1},{1,2},{2,3},{3,4},{4,5},{5,6},{6,7},{7,0},{8,9},{9,10},{10,1... | collective-permute-start | bytes 196616 | tf_op jit(solution)/shard_map/ppermute | solution.py:47
  82.2 7.0 %collective-permute-start.4 = (bf16[128,256]{1,0:T(8,128)(2,1)S(1)}, bf16[128,256]{1,0:T(8,128)(2,1)S(1)}, u32[]{:S(2)}, u32[]{:S(2)}) collective-permute-start(bf16[128,256]{1,0:T(8,128)(2,1)S(1)} %get-tuple-element.24), channel_id=1, source_target_pairs={{0,3},{1,4},{2,5},{3,6},{4,7},{5,0},{6,1},{7,2},{8,11},{9,12},{10,... | collective-permute-start | bytes 196616 | tf_op jit(solution)/shard_map/ppermute | solution.py:47
  90.9 3.9 %collective-permute-start.5 = (bf16[128,256]{1,0:T(8,128)(2,1)S(1)}, bf16[128,256]{1,0:T(8,128)(2,1)S(1)}, u32[]{:S(2)}, u32[]{:S(2)}) collective-permute-start(bf16[128,256]{1,0:T(8,128)(2,1)S(1)} %get-tuple-element.25), channel_id=1, source_target_pairs={{0,4},{1,5},{2,6},{3,7},{4,0},{5,1},{6,2},{7,3},{8,12},{9,13},{10,... | collective-permute-start | bytes 196616 | tf_op jit(solution)/shard_map/ppermute | solution.py:47
  94.9 2.5 %collective-permute-done.2.refs_1_ = bf16[128,256]{1,0:T(8,128)(2,1)S(1)} collective-permute-done((bf16[128,256]{1,0:T(8,128)(2,1)S(1)}, bf16[128,256]{1,0:T(8,128)(2,1)S(1)}, u32[]{:S(2)}, u32[]{:S(2)}) %collective-permute-start.2) | collective-permute-done | bytes 65568 | tf_op jit(solution)/shard_map/ppermute | solution.py:47
  97.3 8.7 %collective-permute-start.6 = (bf16[128,256]{1,0:T(8,128)(2,1)S(1)}, bf16[128,256]{1,0:T(8,128)(2,1)S(1)}, u32[]{:S(2)}, u32[]{:S(2)}) collective-permute-start(bf16[128,256]{1,0:T(8,128)(2,1)S(1)} %get-tuple-element.26), channel_id=1, source_target_pairs={{0,5},{1,6},{2,7},{3,0},{4,1},{5,2},{6,3},{7,4},{8,13},{9,14},{10,... | collective-permute-start | bytes 196616 | tf_op jit(solution)/shard_map/ppermute | solution.py:47
  106.0 20.3 %collective-permute-done.3.refs_2_ = bf16[128,256]{1,0:T(8,128)(2,1)S(1)} collective-permute-done((bf16[128,256]{1,0:T(8,128)(2,1)S(1)}, bf16[128,256]{1,0:T(8,128)(2,1)S(1)}, u32[]{:S(2)}, u32[]{:S(2)}) %collective-permute-start.3) | collective-permute-done | bytes 65568 | tf_op jit(solution)/shard_map/ppermute | solution.py:47
  130.2 5.2 %collective-permute-done.7.refs_6_ = bf16[128,256]{1,0:T(8,128)(2,1)S(1)} collective-permute-done((bf16[128,256]{1,0:T(8,128)(2,1)S(1)}, bf16[128,256]{1,0:T(8,128)(2,1)S(1)}, u32[]{:S(2)}, u32[]{:S(2)}) %collective-permute-start.7) | collective-permute-done | bytes 65568 | tf_op jit(solution)/shard_map/ppermute | solution.py:47
  135.6 3.6 %collective-permute-start.9 = (bf16[8,128,256]{2,1,0:T(8,128)(2,1)S(1)}, bf16[8,128,256]{2,1,0:T(8,128)(2,1)}, u32[]{:S(2)}, u32[]{:S(2)}) collective-permute-start(bf16[8,128,256]{2,1,0:T(8,128)(2,1)S(1)} %merge_keys.1.own_ref), channel_id=1, source_target_pairs={{0,1},{1,2},{2,3},{3,4},{4,5},{5,6},{6,7},{7,8},{8,9},{9,10},{10,1... | collective-permute-start | bytes 1572872 | tf_op jit(solution)/shard_map/ppermute | solution.py:51
  140.4 10.4 %all-to-all-start.2 = ((bf16[32,16,512]{2,1,0:T(8,128)(2,1)}), bf16[32,16,512]{2,1,0:T(8,128)(2,1)S(1)}, u32[]{:S(2)}, u32[]{:S(2)}) async-start(bf16[32,16,512]{2,1,0:T(8,128)(2,1)} %bitcast.32), calls=%async_computation.2 | async-start | bytes 1048576 | tf_op jit(solution)/shard_map/all_to_all | solution.py:56
  150.8 8.2 %collective-permute-done.9.one_ref = bf16[8,128,256]{2,1,0:T(8,128)(2,1)} collective-permute-done((bf16[8,128,256]{2,1,0:T(8,128)(2,1)S(1)}, bf16[8,128,256]{2,1,0:T(8,128)(2,1)}, u32[]{:S(2)}, u32[]{:S(2)}) %collective-permute-start.9) | collective-permute-done | bytes 524320 | tf_op jit(solution)/shard_map/ppermute | solution.py:51
  160.9 5.0 %all-to-all-done.2 = bf16[32,16,512]{2,1,0:T(8,128)(2,1)S(1)} async-done(((bf16[32,16,512]{2,1,0:T(8,128)(2,1)}), bf16[32,16,512]{2,1,0:T(8,128)(2,1)S(1)}, u32[]{:S(2)}, u32[]{:S(2)}) %all-to-all-start.2) | async-done | bytes 524320 | tf_op jit(solution)/shard_map/all_to_all | solution.py:56
  172.2 10.9 %collective-permute-start.17 = (bf16[128,512]{1,0:T(8,128)(2,1)}, bf16[128,512]{1,0:T(8,128)(2,1)S(1)}, u32[]{:S(2)}, u32[]{:S(2)}) collective-permute-start(bf16[128,512]{1,0:T(8,128)(2,1)} %get-tuple-element.35), channel_id=1, source_target_pairs={{0,3},{1,4},{2,5},{3,6},{4,7},{5,0},{6,1},{7,2},{8,11},{9,12},{10,... | collective-permute-start | bytes 393224 | tf_op jit(solution)/shard_map/ppermute | solution.py:47
  188.2 3.7 %collective-permute-start.12 = (bf16[128,512]{1,0:T(8,128)(2,1)}, bf16[128,512]{1,0:T(8,128)(2,1)S(1)}, u32[]{:S(2)}, u32[]{:S(2)}) collective-permute-start(bf16[128,512]{1,0:T(8,128)(2,1)} %copy-done.5), channel_id=1, source_target_pairs={{0,2},{1,3},{2,4},{3,5},{4,6},{5,7},{6,0},{7,1},{8,10},{9,11},{10,... | collective-permute-start | bytes 393224 | tf_op jit(solution)/shard_map/ppermute | solution.py:47
  191.8 7.3 %collective-permute-start.13 = (bf16[128,512]{1,0:T(8,128)(2,1)}, bf16[128,512]{1,0:T(8,128)(2,1)S(1)}, u32[]{:S(2)}, u32[]{:S(2)}) collective-permute-start(bf16[128,512]{1,0:T(8,128)(2,1)} %copy-done.4), channel_id=1, source_target_pairs={{0,6},{1,7},{2,0},{3,1},{4,2},{5,3},{6,4},{7,5},{8,14},{9,15},{10,... | collective-permute-start | bytes 393224 | tf_op jit(solution)/shard_map/ppermute | solution.py:47
  199.2 14.1 %collective-permute-done.17.refs_2_ = bf16[128,512]{1,0:T(8,128)(2,1)S(1)} collective-permute-done((bf16[128,512]{1,0:T(8,128)(2,1)}, bf16[128,512]{1,0:T(8,128)(2,1)S(1)}, u32[]{:S(2)}, u32[]{:S(2)}) %collective-permute-start.17) | collective-permute-done | bytes 131104 | tf_op jit(solution)/shard_map/ppermute | solution.py:47
  215.2 10.1 %collective-permute-start.15 = (bf16[128,512]{1,0:T(8,128)(2,1)}, bf16[128,512]{1,0:T(8,128)(2,1)}, u32[]{:S(2)}, u32[]{:S(2)}) collective-permute-start(bf16[128,512]{1,0:T(8,128)(2,1)} %copy-done.2), channel_id=1, source_target_pairs={{0,7},{1,0},{2,1},{3,2},{4,3},{5,4},{6,5},{7,6},{8,15},{9,8},{10,9... | collective-permute-start | bytes 393224 | tf_op jit(solution)/shard_map/ppermute | solution.py:47
  225.6 5.5 %attend.2.refs_4_ = bf16[4,128,512]{2,1,0:T(8,128)(2,1)S(1)} custom-call(s32[1]{0:T(128)} %bitcast.zl_ref, s32[1,1024]{1,0:T(1,128)S(1)} %pad_add_fusion.landing_ref, s32[128,1]{1,0:T(8,128)S(1)} %copy.15.qdoc_ref, s32[1,384]{1,0:T(1,128)S(1)} %reshape.111.kdoc_ref, bf16[8,128,768]{2,1,0:T(8,128)(2,1)S(1)} %bitcast.23, ...), custom_call_target="tpu_custom_call" | custom-call | tf_op jit(solution)/shard_map/attend/pallas_call | solution.py:182
  231.2 5.6 %attend.3 = bf16[8,128,512]{2,1,0:T(8,128)(2,1)S(1)} custom-call(s32[1]{0:T(128)} %bitcast.zl_ref, s32[1,1024]{1,0:T(1,128)S(1)} %pad_add_fusion.landing_ref, s32[128,1]{1,0:T(8,128)S(1)} %copy.15.qdoc_ref, s32[1,384]{1,0:T(1,128)S(1)} %reshape.111.kdoc_ref, bf16[8,128,768]{2,1,0:T(8,128)(2,1)S(1)} %bitcast.24, ...), custom_call_target="tpu_custom_call" | custom-call | tf_op jit(solution)/shard_map/attend/pallas_call | solution.py:182
  (65 shorter events, 33.9 us)
Async XLA Ops:
  0.0 33.2 %copy-start = (bf16[512,1,768]{2,0,1:T(8,128)(2,1)S(1)}, bf16[512,1,768]{2,0,1:T(8,128)(2,1)}, u32[]{:S(2)}) copy-start(bf16[512,1,768]{2,0,1:T(8,128)(2,1)} %param.5) | copy-start | bytes 2359300
  1.0 21.5 %collective-permute-start.1 = (bf16[512,256]{1,0:T(8,128)(2,1)S(1)}, bf16[512,256]{1,0:T(8,128)(2,1)S(1)}, u32[]{:S(2)}, u32[]{:S(2)}) collective-permute-start(bf16[512,256]{1,0:T(8,128)(2,1)S(1)} %slice.12), channel_id=1, source_target_pairs={{0,64},{1,65},{2,66},{3,67},{4,68},{5,69},{6,70},{7,71},{8,72},{9,... | collective-permute-start | bytes 786440 | tf_op jit(solution)/shard_map/ppermute | solution.py:43
  23.6 18.4 %all-to-all-start.1 = ((bf16[32,16,256]{2,1,0:T(8,128)(2,1)}), bf16[32,16,256]{2,1,0:T(8,128)(2,1)S(1)}, u32[]{:S(2)}, u32[]{:S(2)}) async-start(bf16[32,16,256]{2,1,0:T(8,128)(2,1)} %bitcast.12), calls=%async_computation.1 | async-start | bytes 524288 | tf_op jit(solution)/shard_map/all_to_all | solution.py:56
  42.0 18.1 %all-to-all-start = ((bf16[32,16,768]{2,1,0:T(8,128)(2,1)}), bf16[32,16,768]{2,1,0:T(8,128)(2,1)S(1)}, u32[]{:S(2)}, u32[]{:S(2)}) async-start(bf16[32,16,768]{2,1,0:T(8,128)(2,1)} %bitcast.8), calls=%async_computation | async-start | bytes 1572864 | tf_op jit(solution)/shard_map/all_to_all | solution.py:56
  46.6 92.6 %collective-permute-start.11 = (bf16[512,512]{1,0:T(8,128)(2,1)}, bf16[512,512]{1,0:T(8,128)(2,1)S(1)}, u32[]{:S(2)}, u32[]{:S(2)}) collective-permute-start(bf16[512,512]{1,0:T(8,128)(2,1)} %slice.13), channel_id=1, source_target_pairs={{0,64},{1,65},{2,66},{3,67},{4,68},{5,69},{6,70},{7,71},{8,72},{9,... | collective-permute-start | bytes 1572872 | tf_op jit(solution)/shard_map/ppermute | solution.py:43
  60.8 36.5 %collective-permute-start.2 = (bf16[128,256]{1,0:T(8,128)(2,1)S(1)}, bf16[128,256]{1,0:T(8,128)(2,1)S(1)}, u32[]{:S(2)}, u32[]{:S(2)}) collective-permute-start(bf16[128,256]{1,0:T(8,128)(2,1)S(1)} %get-tuple-element.22), channel_id=1, source_target_pairs={{0,1},{1,2},{2,3},{3,4},{4,5},{5,6},{6,7},{7,0},{8,9},{9,10},{10,1... | collective-permute-start | bytes 196616 | tf_op jit(solution)/shard_map/ppermute | solution.py:47
  80.2 46.1 %collective-permute-start.3 = (bf16[128,256]{1,0:T(8,128)(2,1)S(1)}, bf16[128,256]{1,0:T(8,128)(2,1)S(1)}, u32[]{:S(2)}, u32[]{:S(2)}) collective-permute-start(bf16[128,256]{1,0:T(8,128)(2,1)S(1)} %get-tuple-element.23), channel_id=1, source_target_pairs={{0,2},{1,3},{2,4},{3,5},{4,6},{5,7},{6,0},{7,1},{8,10},{9,11},{10,... | collective-permute-start | bytes 196616 | tf_op jit(solution)/shard_map/ppermute | solution.py:47
  82.2 46.0 %collective-permute-start.4 = (bf16[128,256]{1,0:T(8,128)(2,1)S(1)}, bf16[128,256]{1,0:T(8,128)(2,1)S(1)}, u32[]{:S(2)}, u32[]{:S(2)}) collective-permute-start(bf16[128,256]{1,0:T(8,128)(2,1)S(1)} %get-tuple-element.24), channel_id=1, source_target_pairs={{0,3},{1,4},{2,5},{3,6},{4,7},{5,0},{6,1},{7,2},{8,11},{9,12},{10,... | collective-permute-start | bytes 196616 | tf_op jit(solution)/shard_map/ppermute | solution.py:47
  90.9 39.3 %collective-permute-start.5 = (bf16[128,256]{1,0:T(8,128)(2,1)S(1)}, bf16[128,256]{1,0:T(8,128)(2,1)S(1)}, u32[]{:S(2)}, u32[]{:S(2)}) collective-permute-start(bf16[128,256]{1,0:T(8,128)(2,1)S(1)} %get-tuple-element.25), channel_id=1, source_target_pairs={{0,4},{1,5},{2,6},{3,7},{4,0},{5,1},{6,2},{7,3},{8,12},{9,13},{10,... | collective-permute-start | bytes 196616 | tf_op jit(solution)/shard_map/ppermute | solution.py:47
  97.3 32.9 %collective-permute-start.6 = (bf16[128,256]{1,0:T(8,128)(2,1)S(1)}, bf16[128,256]{1,0:T(8,128)(2,1)S(1)}, u32[]{:S(2)}, u32[]{:S(2)}) collective-permute-start(bf16[128,256]{1,0:T(8,128)(2,1)S(1)} %get-tuple-element.26), channel_id=1, source_target_pairs={{0,5},{1,6},{2,7},{3,0},{4,1},{5,2},{6,3},{7,4},{8,13},{9,14},{10,... | collective-permute-start | bytes 196616 | tf_op jit(solution)/shard_map/ppermute | solution.py:47
  126.3 9.1 %collective-permute-start.7 = (bf16[128,256]{1,0:T(8,128)(2,1)S(1)}, bf16[128,256]{1,0:T(8,128)(2,1)S(1)}, u32[]{:S(2)}, u32[]{:S(2)}) collective-permute-start(bf16[128,256]{1,0:T(8,128)(2,1)S(1)} %get-tuple-element.27), channel_id=1, source_target_pairs={{0,6},{1,7},{2,0},{3,1},{4,2},{5,3},{6,4},{7,5},{8,14},{9,15},{10,... | collective-permute-start | bytes 196616 | tf_op jit(solution)/shard_map/ppermute | solution.py:47
  128.2 7.2 %collective-permute-start.8 = (bf16[128,256]{1,0:T(8,128)(2,1)S(1)}, bf16[128,256]{1,0:T(8,128)(2,1)S(1)}, u32[]{:S(2)}, u32[]{:S(2)}) collective-permute-start(bf16[128,256]{1,0:T(8,128)(2,1)S(1)} %get-tuple-element.28), channel_id=1, source_target_pairs={{0,7},{1,0},{2,1},{3,2},{4,3},{5,4},{6,5},{7,6},{8,15},{9,8},{10,9... | collective-permute-start | bytes 196616 | tf_op jit(solution)/shard_map/ppermute | solution.py:47
  135.6 49.5 %copy-start.6 = (s32[1024]{0:T(1024)S(1)}, s32[1024]{0:T(1024)}, u32[]{:S(2)}) copy-start(s32[1024]{0:T(1024)} %param.7) | copy-start | bytes 12292
  135.6 23.4 %collective-permute-start.9 = (bf16[8,128,256]{2,1,0:T(8,128)(2,1)S(1)}, bf16[8,128,256]{2,1,0:T(8,128)(2,1)}, u32[]{:S(2)}, u32[]{:S(2)}) collective-permute-start(bf16[8,128,256]{2,1,0:T(8,128)(2,1)S(1)} %merge_keys.1.own_ref), channel_id=1, source_target_pairs={{0,1},{1,2},{2,3},{3,4},{4,5},{5,6},{6,7},{7,8},{8,9},{9,10},{10,1... | collective-permute-start | bytes 1572872 | tf_op jit(solution)/shard_map/ppermute | solution.py:51
  140.4 25.4 %all-to-all-start.2 = ((bf16[32,16,512]{2,1,0:T(8,128)(2,1)}), bf16[32,16,512]{2,1,0:T(8,128)(2,1)S(1)}, u32[]{:S(2)}, u32[]{:S(2)}) async-start(bf16[32,16,512]{2,1,0:T(8,128)(2,1)} %bitcast.32), calls=%async_computation.2 | async-start | bytes 1048576 | tf_op jit(solution)/shard_map/all_to_all | solution.py:56
  159.0 66.6 %collective-permute-start.10 = (bf16[8,128,256]{2,1,0:T(8,128)(2,1)}, bf16[8,128,256]{2,1,0:T(8,128)(2,1)}, u32[]{:S(2)}, u32[]{:S(2)}) collective-permute-start(bf16[8,128,256]{2,1,0:T(8,128)(2,1)} %collective-permute-done.9.one_ref), channel_id=1, source_target_pairs={{0,1},{1,2},{2,3},{3,4},{4,5},{5,6},{6,7},{7,8},{8,9},{9,10},{10,1... | collective-permute-start | bytes 1572872 | tf_op jit(solution)/shard_map/ppermute | solution.py:51
  170.3 21.5 %collective-permute-start.16 = (bf16[128,512]{1,0:T(8,128)(2,1)}, bf16[128,512]{1,0:T(8,128)(2,1)S(1)}, u32[]{:S(2)}, u32[]{:S(2)}) collective-permute-start(bf16[128,512]{1,0:T(8,128)(2,1)} %get-tuple-element.34), channel_id=1, source_target_pairs={{0,4},{1,5},{2,6},{3,7},{4,0},{5,1},{6,2},{7,3},{8,12},{9,13},{10,... | collective-permute-start | bytes 393224 | tf_op jit(solution)/shard_map/ppermute | solution.py:47
  172.2 41.0 %collective-permute-start.17 = (bf16[128,512]{1,0:T(8,128)(2,1)}, bf16[128,512]{1,0:T(8,128)(2,1)S(1)}, u32[]{:S(2)}, u32[]{:S(2)}) collective-permute-start(bf16[128,512]{1,0:T(8,128)(2,1)} %get-tuple-element.35), channel_id=1, source_target_pairs={{0,3},{1,4},{2,5},{3,6},{4,7},{5,0},{6,1},{7,2},{8,11},{9,12},{10,... | collective-permute-start | bytes 393224 | tf_op jit(solution)/shard_map/ppermute | solution.py:47
  183.2 32.0 %collective-permute-start.18 = (bf16[128,512]{1,0:T(8,128)(2,1)}, bf16[128,512]{1,0:T(8,128)(2,1)S(1)}, u32[]{:S(2)}, u32[]{:S(2)}) collective-permute-start(bf16[128,512]{1,0:T(8,128)(2,1)} %get-tuple-element.36), channel_id=1, source_target_pairs={{0,5},{1,6},{2,7},{3,0},{4,1},{5,2},{6,3},{7,4},{8,13},{9,14},{10,... | collective-permute-start | bytes 393224 | tf_op jit(solution)/shard_map/ppermute | solution.py:47
  185.1 3.0 %collective-permute-start = (s32[256]{0:T(256)S(1)}, s32[256]{0:T(256)S(1)}, u32[]{:S(2)}, u32[]{:S(2)}) collective-permute-start(s32[256]{0:T(256)S(1)} %slice.9), channel_id=1, source_target_pairs={{0,8},{1,9},{2,10},{3,11},{4,12},{5,13},{6,14},{7,15},{8,16},{9,17... | collective-permute-start | bytes 3080 | tf_op jit(solution)/shard_map/ppermute | solution.py:51
  188.2 43.0 %collective-permute-start.12 = (bf16[128,512]{1,0:T(8,128)(2,1)}, bf16[128,512]{1,0:T(8,128)(2,1)S(1)}, u32[]{:S(2)}, u32[]{:S(2)}) collective-permute-start(bf16[128,512]{1,0:T(8,128)(2,1)} %copy-done.5), channel_id=1, source_target_pairs={{0,2},{1,3},{2,4},{3,5},{4,6},{5,7},{6,0},{7,1},{8,10},{9,11},{10,... | collective-permute-start | bytes 393224 | tf_op jit(solution)/shard_map/ppermute | solution.py:47
  191.8 39.3 %collective-permute-start.13 = (bf16[128,512]{1,0:T(8,128)(2,1)}, bf16[128,512]{1,0:T(8,128)(2,1)S(1)}, u32[]{:S(2)}, u32[]{:S(2)}) collective-permute-start(bf16[128,512]{1,0:T(8,128)(2,1)} %copy-done.4), channel_id=1, source_target_pairs={{0,6},{1,7},{2,0},{3,1},{4,2},{5,3},{6,4},{7,5},{8,14},{9,15},{10,... | collective-permute-start | bytes 393224 | tf_op jit(solution)/shard_map/ppermute | solution.py:47
  213.2 17.9 %collective-permute-start.14 = (bf16[128,512]{1,0:T(8,128)(2,1)}, bf16[128,512]{1,0:T(8,128)(2,1)}, u32[]{:S(2)}, u32[]{:S(2)}) collective-permute-start(bf16[128,512]{1,0:T(8,128)(2,1)} %copy-done.3), channel_id=1, source_target_pairs={{0,1},{1,2},{2,3},{3,4},{4,5},{5,6},{6,7},{7,0},{8,9},{9,10},{10,1... | collective-permute-start | bytes 393224 | tf_op jit(solution)/shard_map/ppermute | solution.py:47
  215.2 16.0 %collective-permute-start.15 = (bf16[128,512]{1,0:T(8,128)(2,1)}, bf16[128,512]{1,0:T(8,128)(2,1)}, u32[]{:S(2)}, u32[]{:S(2)}) collective-permute-start(bf16[128,512]{1,0:T(8,128)(2,1)} %copy-done.2), channel_id=1, source_target_pairs={{0,7},{1,0},{2,1},{3,2},{4,3},{5,4},{6,5},{7,6},{8,15},{9,8},{10,9... | collective-permute-start | bytes 393224 | tf_op jit(solution)/shard_map/ppermute | solution.py:47
  (5 other events, 3.4 us)

commit v3 on v1

v3 whole, which is shorter than its diff:
```python
import functools

import jax
import jax.numpy as jnp
import numpy as np
from jax import lax
from jax.experimental import pallas as pl
from jax.experimental.pallas import tpu as pltpu
from jax.sharding import Mesh
from jax.sharding import PartitionSpec as P

HD = 128
QPG = 4
GROUPS = 8
QW = QPG * HD
KW = 2 * HD
PART = 2 * HD
ROWS = 128
SHARD = 1024
SLOTS = 16
SOURCES = 64
PER_SOURCE = 512
COLUMNS = 32
PLANES = 16
REACH = 256
AXES = ("x", "zh", "y", "c", "zl")
SIZES = (4, 2, 4, 2, 8)
COUNT = 512
VMEM = 48 * 1024 * 1024
PLANE_OF = (15, 1, 3, 10, 14, 9, 2, 5, 13, 7, 8, 4, 0, 11, 6, 12)
UNIT_OF = tuple(int(u) for u in np.argsort(np.array(PLANE_OF)))


def flat_id(x, zh, y, c, zl):
    return (((x * 2 + zh) * 4 + y) * 2 + c) * 8 + zl


def to_plane(value, swapped):
    ids = []
    for x in range(4):
        for y in range(4):
            for c in range(2):
                for zh in range(2):
                    for zl in range(8):
                        plane = PLANE_OF[zl * 2 + (zh ^ swapped)]
                        target = flat_id(x, plane // 8, y, c, plane % 8)
                        ids.append((flat_id(x, zh, y, c, zl), target))
    return lax.ppermute(value, AXES, ids)


def from_behind(value, steps):
    return lax.ppermute(value, AXES, [(i, i + steps) for i in range(COUNT - steps)])


def over_columns(slots):
    return lax.all_to_all(slots, ("x", "y", "c"), split_axis=0, concat_axis=0, tiled=True)


def over_planes(blocks):
    return lax.all_to_all(blocks, ("zh", "zl"), split_axis=0, concat_axis=0, tiled=True)


def after(value, *others):
    return lax.optimization_barrier((value, *others))[0]


def vmem():
    return pl.BlockSpec(memory_space=pltpu.VMEM)


def smem():
    return pl.BlockSpec(memory_space=pltpu.SMEM)


def call(kernel, name, out_shape, scalars, *arrays):
    return pl.pallas_call(
        kernel,
        out_shape=out_shape,
        in_specs=[smem()] * len(scalars) + [vmem()] * len(arrays),
        out_specs=vmem(),
        compiler_params=pltpu.CompilerParams(vmem_limit_bytes=VMEM),
        name=name,
    )(*scalars, *arrays)


def bf16(*shape):
    return jax.ShapeDtypeStruct(shape, jnp.bfloat16)


def pick(first, codes, rows):
    wanted = lax.broadcasted_iota(jnp.int32, (ROWS, codes.shape[1]), 0) + first
    onehot = jnp.where(wanted == codes, 1.0, 0.0).astype(jnp.bfloat16)
    return jnp.dot(onehot, rows, preferred_element_type=jnp.float32).astype(jnp.bfloat16)


def slots_kernel(count, *refs):
    codes, sources, out_ref = refs[:count], refs[count : 2 * count], refs[-1]
    for turn in range(count):
        for part in range(SOURCES * SLOTS // ROWS):
            picked = pick(part * ROWS, codes[turn][...], sources[turn][...])
            for i in range(ROWS // SLOTS):
                column, half = (part * (ROWS // SLOTS) + i) // 2, i % 2
                low = (half * count + turn) * SLOTS
                out_ref[column, low : low + SLOTS, :] = picked[i * SLOTS : (i + 1) * SLOTS]


def to_slots(codes, sources):
    count = len(codes)
    shape = bf16(COLUMNS, 2 * count * SLOTS, sources[0].shape[1])
    return call(functools.partial(slots_kernel, count), "to_slots", shape, (), *codes, *sources)


def blocks_kernel(low_land, high_land, slots_ref, out_ref):
    per_half, width = slots_ref.shape[1] // 2, slots_ref.shape[2]
    for half, landing in enumerate((low_land, high_land)):
        slots = slots_ref[:, half * per_half : (half + 1) * per_half, :]
        slots = slots.reshape(COLUMNS * per_half, width)
        for block in range(GROUPS):
            out_ref[half * GROUPS + block] = pick(block * ROWS, landing[...], slots)


def to_blocks(landings, slots):
    return call(blocks_kernel, "to_blocks", bf16(PLANES, ROWS, slots.shape[2]), (), *landings, slots)


def landed(first, landing):
    rows = lax.broadcasted_iota(jnp.int32, (ROWS, landing.shape[1]), 0) + first
    return jnp.max(jnp.where(rows == landing, 1.0, 0.0), axis=1, keepdims=True) > 0.0


def merge_kernel(zl_ref, landing_ref, text_ref, arrived_ref, out_ref):
    present = landed(zl_ref[0] * ROWS, landing_ref[...])
    for group in range(GROUPS):
        arrived = arrived_ref[group] + arrived_ref[GROUPS + group]
        out_ref[group] = jnp.where(present, arrived, text_ref[group, :, QW:])


def merge_keys(zl, landing, text, arrived):
    return call(merge_kernel, "merge_keys", bf16(GROUPS, ROWS, KW), (zl,), landing, text, arrived)


def attend_kernel(zl_ref, landing_ref, qdoc_ref, kdoc_ref, text_ref, two_ref, one_ref, own_ref, arrived_ref, out_ref):
    present = landed(zl_ref[0] * ROWS, landing_ref[...])
    window = REACH + ROWS
    query_pos = lax.broadcasted_iota(jnp.int32, (ROWS, window), 0) + REACH
    key_pos = lax.broadcasted_iota(jnp.int32, (ROWS, window), 1)
    allowed = (kdoc_ref[...] == qdoc_ref[...]) & (key_pos <= query_pos)
    factor = HD ** (-0.5)
    for group in range(GROUPS):
        joined = jnp.concatenate([two_ref[group], one_ref[group], own_ref[group]], 0)
        keys, values = joined[:, :HD], joined[:, HD:]
        queries = []
        for head in range(QPG):
            low = (head % 2) * HD
            arrived = arrived_ref[PLANE_OF[group * 2 + head // 2], :, low : low + HD]
            text = text_ref[group, :, head * HD : (head + 1) * HD]
            queries.append(jnp.where(present, arrived, text))
        scores = lax.dot_general(
            jnp.concatenate(queries, 0),
            keys,
            (((1,), (1,)), ((), ())),
            preferred_element_type=jnp.float32,
        )
        for head in range(QPG):
            masked = jnp.where(allowed, scores[head * ROWS : (head + 1) * ROWS] * factor, -jnp.inf)
            row_max = jnp.max(masked, axis=1, keepdims=True)
            terms = jnp.exp(masked - row_max)
            total = jnp.sum(terms, axis=1, keepdims=True)
            summed = jnp.dot(terms.astype(jnp.bfloat16), values, preferred_element_type=jnp.float32)
            out_ref[group, :, head * HD : (head + 1) * HD] = (summed / total).astype(jnp.bfloat16)


def body(text_rows, vision_rows, vision_pos, doc_ids):
    rows = vision_rows.reshape(PER_SOURCE, QW + KW)
    x, half, y, c, zl = [lax.axis_index(axis) for axis in AXES]
    zl_arr = zl.reshape(1)
    part = jnp.asarray(UNIT_OF, jnp.int32)[half * 8 + zl] % 2
    text = jnp.transpose(text_rows, (1, 0, 2))

    zero, one = rows[:, :PART], rows[:, PART:QW]
    moved = (
        to_plane(jnp.where(half == 0, zero, one), 0),
        to_plane(jnp.where(half == 0, one, zero), 1),
    )

    pos = vision_pos.reshape(SOURCES, PER_SOURCE)
    target = pos // SHARD
    index = jnp.arange(PER_SOURCE, dtype=jnp.int32)

    def code_of(source_half):
        source = ((x * 2 + source_half) * 4 + y) * 2 + c
        own = lax.dynamic_index_in_dim(target, source, 0, keepdims=False)
        same = (own[None, :] == own[:, None]) & (index[:, None] < index[None, :])
        rank = jnp.sum(same.astype(jnp.int32), axis=0)
        column = (own // 16) * 8 + own % 8
        to_half = (own // 8) % 2
        return ((column * 2 + to_half) * SLOTS + rank).reshape(1, PER_SOURCE)

    slot = jnp.arange(SLOTS, dtype=jnp.int32)

    def landing_of(shard_half):
        shard = ((x * 2 + shard_half) * 4 + y) * 2 + c
        hit = target == shard
        skip = jnp.sum((target < shard).astype(jnp.int32), axis=1, keepdims=True)
        rank = jnp.where(hit, index[None, :] - skip, -1)
        chosen = rank[:, None, :] == slot[None, :, None]
        local = pos - shard * SHARD + 1
        landing = jnp.sum(jnp.where(chosen, local[:, None, :], 0), axis=2) - 1
        return jnp.transpose(landing.reshape(4, 2, 8, SLOTS), (0, 2, 1, 3))

    landings = (landing_of(0), landing_of(1))

    def one_source(landing):
        return jnp.where(half == 0, landing[:, :, 0], landing[:, :, 1]).reshape(1, -1)

    def two_sources(landing):
        return jnp.where(part == 0, landing, landing[:, :, ::-1]).reshape(1, -1)

    landing = jnp.where(half == 0, landings[0], landings[1]).reshape(1, -1)

    marks = doc_ids + 1
    joined_marks = jnp.concatenate([from_behind(marks[SHARD - REACH :], 8), marks], 0)
    kdoc = lax.dynamic_slice_in_dim(joined_marks, zl * ROWS, REACH + ROWS).reshape(1, -1)
    qdoc = lax.dynamic_slice_in_dim(marks, zl * ROWS, ROWS).reshape(-1, 1)

    slots_kv = over_columns(to_slots((code_of(half),), (rows[:, QW:],)))
    blocks_kv = to_blocks([one_source(each) for each in landings], after(slots_kv, *moved))
    own_kv = merge_keys(zl_arr, landing, text, over_planes(blocks_kv))
    one_kv = from_behind(own_kv, 1)
    two_kv = from_behind(one_kv, 1)

    slots_q = to_slots((code_of(part), code_of(1 - part)), moved)
    slots_q = over_columns(after(slots_q, own_kv))
    blocks_q = to_blocks([two_sources(each) for each in landings], slots_q)
    arrived_q = over_planes(after(blocks_q, two_kv))

    out = call(
        attend_kernel, "attend", bf16(GROUPS, ROWS, QW),
        (zl_arr,), landing, qdoc, kdoc, text, two_kv, one_kv, own_kv, arrived_q,
    )
    return jnp.transpose(out, (1, 0, 2))


def solution(mesh):
    fine = Mesh(mesh.devices.reshape(SIZES), AXES)
    in_specs = (
        P(AXES, None, None),
        P(("x", "zh", "y", "c"), "zl", None),
        P(),
        P(("x", "zh", "y", "c")),
    )
    return jax.shard_map(
        body, mesh=fine, in_specs=in_specs, out_specs=P(AXES, None, None), check_vma=False
    )
```

time: 238 us -> 208 us (0.87)
  the two profiles are of different devices: /device:TPU:111 before, /device:TPU:104 now
where the time goes in v3:
time: 208 us; the launch traced here: 207 us
  waiting for transfers between devices  107 us (51%)
  starting transfers between devices  77.6 us (37%)
  Pallas kernels  10.5 us (5%)
  local copies, waits for them, and re-layouts  5.59 us (3%)
  other arithmetic  4.49 us (2%)
  between operations  2.25 us (1%)
    all_to_all x2, waiting for transfers between devices, over_planes(): lax.all_to_all(blocks, ('zh', 'zl'), split_axis=0, concat_axis=0, tiled=T...  86.5 us
    all_to_all x2, starting transfers between devices, over_planes(): lax.all_to_all(blocks, ('zh', 'zl'), split_axis=0, concat_axis=0, tiled=T...  38.1 us
    all_to_all x2, starting transfers between devices, over_columns(): lax.all_to_all(slots, ('x', 'y', 'c'), split_axis=0, concat_axis=0, tiled...  14.4 us
    ppermute x2, starting transfers between devices, to_plane(): return lax.ppermute(value, AXES, ids)  14.1 us
    ppermute x3, starting transfers between devices, from_behind(): lax.ppermute(value, AXES, [(i, i + steps) for i in range(COUNT - steps)])  11 us
    pallas_call x6, Pallas kernels, call(): pl.pallas_call(kernel, out_shape=out_shape, in_specs=[smem()] * len(scala...  10.5 us
    ppermute x2, waiting for transfers between devices, to_plane(): return lax.ppermute(value, AXES, ids)  7.93 us
    all_to_all x2, waiting for transfers between devices, over_columns(): lax.all_to_all(slots, ('x', 'y', 'c'), split_axis=0, concat_axis=0, tiled...  7.9 us
  transfers between devices with their start and end apart: 9, of which 6 were waited for; matrix products, arithmetic and copies ran while one was open for 3% of the time, Pallas kernels for 2%

profile of v3, /device:TPU:104, one launch (start us, length us, event | category | flops | bytes accessed | tf_op | source)
XLA Modules:
  0.0 207.0 jit_solution(4197550837160360271)
XLA Ops:
  0.0 1.2 broadcast_select_fusion
  1.2 2.0 collective-permute-start.1
  3.2 12.1 %collective-permute-start.2 = (bf16[512,256]{1,0:T(8,128)(2,1)S(1)}, bf16[512,256]{1,0:T(8,128)(2,1)S(1)}, u32[]{:S(2)}, u32[]{:S(2)}) collective-permute-start(bf16[512,256]{1,0:T(8,128)(2,1)S(1)} %get-tuple-element.14), channel_id=1, source_target_pairs={{0,1},{1,66},{2,65},{3,5},{4,7},{5,4},{6,67},{7,68},{64,71},{65,3}... | collective-permute-start | bytes 786440 | tf_op jit(solution)/shard_map/ppermute | solution.py:48
  18.5 1.2 to_slots.2
  19.7 7.5 %all-to-all-start = ((bf16[32,32,256]{2,1,0:T(8,128)(2,1)}), bf16[32,32,256]{2,1,0:T(8,128)(2,1)S(1)}, u32[]{:S(2)}, u32[]{:S(2)}) async-start(bf16[32,32,256]{2,1,0:T(8,128)(2,1)} %to_slots.2), calls=%async_computation | async-start | bytes 1048576 | tf_op jit(solution)/shard_map/all_to_all | solution.py:56
  27.3 2.2 %select_reduce_fusion = (s32[64,16]{1,0:T(8,128)S(1)}, s32[64,16]{1,0:T(8,128)S(1)}) fusion(s32[64,512]{1,0:T(8,128)S(1)} %get-tuple-element.22, s32[64,512]{1,0:T(8,128)S(1)} %get-tuple-element.20, s32[64,512]{1,0:T(8,128)S(1)} %get-tuple-element.23, s32[64,512]{1,0:T(8,128)S(1)} %get-tuple-element.21), kind=kLoop, calls=%fused_computation | loop fusion | flops 3143680 | bytes 532480 | tf_op jit(solution)/shard_map/reduce_sum | solution.py:208
  29.8 7.9 %collective-permute-done.2.refs_3_ = bf16[512,256]{1,0:T(8,128)(2,1)S(1)} collective-permute-done((bf16[512,256]{1,0:T(8,128)(2,1)S(1)}, bf16[512,256]{1,0:T(8,128)(2,1)S(1)}, u32[]{:S(2)}, u32[]{:S(2)}) %collective-permute-start.2) | collective-permute-done | bytes 262176 | tf_op jit(solution)/shard_map/ppermute | solution.py:48
  37.7 1.7 to_blocks.2
  39.4 10.4 %all-to-all-start.1 = ((bf16[16,128,256]{2,1,0:T(8,128)(2,1)}), bf16[16,128,256]{2,1,0:T(8,128)(2,1)S(1)}, u32[]{:S(2)}, u32[]{:S(2)}) async-start(bf16[16,128,256]{2,1,0:T(8,128)(2,1)} %to_blocks.2), calls=%async_computation.1 | async-start | bytes 2097152 | tf_op jit(solution)/shard_map/all_to_all | solution.py:60
  50.0 1.7 copy.22
  52.0 45.8 %all-to-all-done.1.arrived_ref = bf16[16,128,256]{2,1,0:T(8,128)(2,1)S(1)} async-done(((bf16[16,128,256]{2,1,0:T(8,128)(2,1)}), bf16[16,128,256]{2,1,0:T(8,128)(2,1)S(1)}, u32[]{:S(2)}, u32[]{:S(2)}) %all-to-all-start.1) | async-done | bytes 1048608 | tf_op jit(solution)/shard_map/all_to_all | solution.py:60
  98.0 3.2 %collective-permute-start.3 = (bf16[8,128,256]{2,1,0:T(8,128)(2,1)S(1)}, bf16[8,128,256]{2,1,0:T(8,128)(2,1)}, u32[]{:S(2)}, u32[]{:S(2)}) collective-permute-start(bf16[8,128,256]{2,1,0:T(8,128)(2,1)S(1)} %merge_keys.1.own_ref), channel_id=1, source_target_pairs={{0,1},{1,2},{2,3},{3,4},{4,5},{5,6},{6,7},{7,8},{8,9},{9,10},{10,1... | collective-permute-start | bytes 1572872 | tf_op jit(solution)/shard_map/ppermute | solution.py:52
  102.0 1.0 copy-done
  102.9 6.9 %all-to-all-start.2 = ((bf16[32,64,256]{2,1,0:T(8,128)(2,1)}), bf16[32,64,256]{2,1,0:T(8,128)(2,1)S(1)}, u32[]{:S(2)}, u32[]{:S(2)}) async-start(bf16[32,64,256]{2,1,0:T(8,128)(2,1)} %copy-done), calls=%async_computation.2 | async-start | bytes 2097152 | tf_op jit(solution)/shard_map/all_to_all | solution.py:56
  109.8 1.7 collective-permute-done.3.one_ref
  111.5 5.7 %collective-permute-start.4 = (bf16[8,128,256]{2,1,0:T(8,128)(2,1)}, bf16[8,128,256]{2,1,0:T(8,128)(2,1)}, u32[]{:S(2)}, u32[]{:S(2)}) collective-permute-start(bf16[8,128,256]{2,1,0:T(8,128)(2,1)} %collective-permute-done.3.one_ref), channel_id=1, source_target_pairs={{0,1},{1,2},{2,3},{3,4},{4,5},{5,6},{6,7},{7,8},{8,9},{9,10},{10,1... | collective-permute-start | bytes 1572872 | tf_op jit(solution)/shard_map/ppermute | solution.py:52
  117.5 7.9 %all-to-all-done.2.slots_ref = bf16[32,64,256]{2,1,0:T(8,128)(2,1)S(1)} async-done(((bf16[32,64,256]{2,1,0:T(8,128)(2,1)}), bf16[32,64,256]{2,1,0:T(8,128)(2,1)S(1)}, u32[]{:S(2)}, u32[]{:S(2)}) %all-to-all-start.2) | async-done | bytes 1048608 | tf_op jit(solution)/shard_map/all_to_all | solution.py:56
  125.4 2.2 %to_blocks.3 = bf16[16,128,256]{2,1,0:T(8,128)(2,1)} custom-call(s32[1,1024]{1,0:T(1,128)S(1)} %reshape.177.low_land, s32[1,1024]{1,0:T(1,128)S(1)} %reshape.178.high_land, bf16[32,64,256]{2,1,0:T(8,128)(2,1)S(1)} %all-to-all-done.2.slots_ref), custom_call_target="tpu_custom_call" | custom-call | tf_op jit(solution)/shard_map/to_blocks/pallas_call | solution.py:76
  127.6 27.7 %all-to-all-start.3 = ((bf16[16,128,256]{2,1,0:T(8,128)(2,1)}), bf16[16,128,256]{2,1,0:T(8,128)(2,1)S(1)}, u32[]{:S(2)}, u32[]{:S(2)}) async-start(bf16[16,128,256]{2,1,0:T(8,128)(2,1)} %to_blocks.3), calls=%async_computation.3 | async-start | bytes 2097152 | tf_op jit(solution)/shard_map/all_to_all | solution.py:60
  155.4 2.1 %collective-permute-start = (s32[256]{0:T(256)S(1)}, s32[256]{0:T(256)S(1)}, u32[]{:S(2)}, u32[]{:S(2)}) collective-permute-start(s32[256]{0:T(256)S(1)} %slice.24), channel_id=1, source_target_pairs={{0,8},{1,9},{2,10},{3,11},{4,12},{5,13},{6,14},{7,15},{8,16},{9,17... | collective-permute-start | bytes 3080 | tf_op jit(solution)/shard_map/ppermute | solution.py:52
  157.7 2.6 %collective-permute-done = s32[256]{0:T(256)S(1)} collective-permute-done((s32[256]{0:T(256)S(1)}, s32[256]{0:T(256)S(1)}, u32[]{:S(2)}, u32[]{:S(2)}) %collective-permute-start) | collective-permute-done | bytes 1056 | tf_op jit(solution)/shard_map/ppermute | solution.py:52
  160.3 40.7 %all-to-all-done.3.arrived_ref = bf16[16,128,256]{2,1,0:T(8,128)(2,1)S(1)} async-done(((bf16[16,128,256]{2,1,0:T(8,128)(2,1)}), bf16[16,128,256]{2,1,0:T(8,128)(2,1)S(1)}, u32[]{:S(2)}, u32[]{:S(2)}) %all-to-all-start.3) | async-done | bytes 1048608 | tf_op jit(solution)/shard_map/all_to_all | solution.py:60
  201.0 4.4 %attend.1 = bf16[8,128,512]{2,1,0:T(8,128)(2,1)S(1)} custom-call(s32[1]{0:T(128)} %bitcast.zl_ref, s32[1,1024]{1,0:T(1,128)S(1)} %reshape.173.landing_ref, s32[128,1]{1,0:T(8,128)S(1)} %copy.19.qdoc_ref, s32[1,384]{1,0:T(1,128)S(1)} %reshape.175.kdoc_ref, bf16[8,128,768]{2,1,0:T(8,128)(2,1)S(1)} %bitcast.30, ...), custom_call_target="tpu_custom_call" | custom-call | tf_op jit(solution)/shard_map/attend/pallas_call | solution.py:76
  205.4 1.5 copy.20
  (45 shorter events, 3.3 us)
Async XLA Ops:
  0.0 15.4 %copy-start.5 = (s32[16]{0:T(128)S(1)}, s32[16]{0:T(128)}, u32[]{:S(2)}) copy-start(s32[16]{0:T(128)} %constant.167.clone) | copy-start | bytes 196
  0.0 18.0 %copy-start.3 = (s32[32768]{0:T(1024)S(1)}, s32[32768]{0:T(1024)}, u32[]{:S(2)}) copy-start(s32[32768]{0:T(1024)} %param.7) | copy-start | bytes 393220
  1.2 28.6 %collective-permute-start.1 = (bf16[512,256]{1,0:T(8,128)(2,1)S(1)}, bf16[512,256]{1,0:T(8,128)(2,1)S(1)}, u32[]{:S(2)}, u32[]{:S(2)}) collective-permute-start(bf16[512,256]{1,0:T(8,128)(2,1)S(1)} %get-tuple-element.16), channel_id=1, source_target_pairs={{0,71},{1,3},{2,70},{3,2},{4,69},{5,64},{6,0},{7,6},{64,1},{65,66}... | collective-permute-start | bytes 786440 | tf_op jit(solution)/shard_map/ppermute | solution.py:48
  3.2 34.5 %collective-permute-start.2 = (bf16[512,256]{1,0:T(8,128)(2,1)S(1)}, bf16[512,256]{1,0:T(8,128)(2,1)S(1)}, u32[]{:S(2)}, u32[]{:S(2)}) collective-permute-start(bf16[512,256]{1,0:T(8,128)(2,1)S(1)} %get-tuple-element.14), channel_id=1, source_target_pairs={{0,1},{1,66},{2,65},{3,5},{4,7},{5,4},{6,67},{7,68},{64,71},{65,3}... | collective-permute-start | bytes 786440 | tf_op jit(solution)/shard_map/ppermute | solution.py:48
  19.7 18.0 %all-to-all-start = ((bf16[32,32,256]{2,1,0:T(8,128)(2,1)}), bf16[32,32,256]{2,1,0:T(8,128)(2,1)S(1)}, u32[]{:S(2)}, u32[]{:S(2)}) async-start(bf16[32,32,256]{2,1,0:T(8,128)(2,1)} %to_slots.2), calls=%async_computation | async-start | bytes 1048576 | tf_op jit(solution)/shard_map/all_to_all | solution.py:56
  37.7 1.7 copy-start.1
  39.4 58.4 %all-to-all-start.1 = ((bf16[16,128,256]{2,1,0:T(8,128)(2,1)}), bf16[16,128,256]{2,1,0:T(8,128)(2,1)S(1)}, u32[]{:S(2)}, u32[]{:S(2)}) async-start(bf16[16,128,256]{2,1,0:T(8,128)(2,1)} %to_blocks.2), calls=%async_computation.1 | async-start | bytes 2097152 | tf_op jit(solution)/shard_map/all_to_all | solution.py:60
  97.8 3.4 %copy-start.2 = (bf16[512,256]{1,0:T(8,128)(2,1)S(1)}, bf16[512,256]{1,0:T(8,128)(2,1)}, u32[]{:S(2)}) copy-start(bf16[512,256]{1,0:T(8,128)(2,1)} %copy-done.1) | copy-start | bytes 786436
  98.0 13.5 %collective-permute-start.3 = (bf16[8,128,256]{2,1,0:T(8,128)(2,1)S(1)}, bf16[8,128,256]{2,1,0:T(8,128)(2,1)}, u32[]{:S(2)}, u32[]{:S(2)}) collective-permute-start(bf16[8,128,256]{2,1,0:T(8,128)(2,1)S(1)} %merge_keys.1.own_ref), channel_id=1, source_target_pairs={{0,1},{1,2},{2,3},{3,4},{4,5},{5,6},{6,7},{7,8},{8,9},{9,10},{10,1... | collective-permute-start | bytes 1572872 | tf_op jit(solution)/shard_map/ppermute | solution.py:52
  102.0 1.0 copy-start
  102.9 22.4 %all-to-all-start.2 = ((bf16[32,64,256]{2,1,0:T(8,128)(2,1)}), bf16[32,64,256]{2,1,0:T(8,128)(2,1)S(1)}, u32[]{:S(2)}, u32[]{:S(2)}) async-start(bf16[32,64,256]{2,1,0:T(8,128)(2,1)} %copy-done), calls=%async_computation.2 | async-start | bytes 2097152 | tf_op jit(solution)/shard_map/all_to_all | solution.py:56
  111.5 16.1 %collective-permute-start.4 = (bf16[8,128,256]{2,1,0:T(8,128)(2,1)}, bf16[8,128,256]{2,1,0:T(8,128)(2,1)}, u32[]{:S(2)}, u32[]{:S(2)}) collective-permute-start(bf16[8,128,256]{2,1,0:T(8,128)(2,1)} %collective-permute-done.3.one_ref), channel_id=1, source_target_pairs={{0,1},{1,2},{2,3},{3,4},{4,5},{5,6},{6,7},{7,8},{8,9},{9,10},{10,1... | collective-permute-start | bytes 1572872 | tf_op jit(solution)/shard_map/ppermute | solution.py:52
  127.6 27.7 %copy-start.4 = (s32[1024]{0:T(1024)S(1)}, s32[1024]{0:T(1024)}, u32[]{:S(2)}) copy-start(s32[1024]{0:T(1024)} %param.8) | copy-start | bytes 12292
  127.6 73.4 %all-to-all-start.3 = ((bf16[16,128,256]{2,1,0:T(8,128)(2,1)}), bf16[16,128,256]{2,1,0:T(8,128)(2,1)S(1)}, u32[]{:S(2)}, u32[]{:S(2)}) async-start(bf16[16,128,256]{2,1,0:T(8,128)(2,1)} %to_blocks.3), calls=%async_computation.3 | async-start | bytes 2097152 | tf_op jit(solution)/shard_map/all_to_all | solution.py:60
  155.4 4.9 %collective-permute-start = (s32[256]{0:T(256)S(1)}, s32[256]{0:T(256)S(1)}, u32[]{:S(2)}, u32[]{:S(2)}) collective-permute-start(s32[256]{0:T(256)S(1)} %slice.24), channel_id=1, source_target_pairs={{0,8},{1,9},{2,10},{3,11},{4,12},{5,13},{6,14},{7,15},{8,16},{9,17... | collective-permute-start | bytes 3080 | tf_op jit(solution)/shard_map/ppermute | solution.py:52

commit v4 on v3

--- a/solution.py
+++ b/solution.py
@@ -77,7 +77,7 @@
         kernel,
         out_shape=out_shape,
         in_specs=[smem()] * len(scalars) + [vmem()] * len(arrays),
-        out_specs=vmem(),
+        out_specs=[vmem()] * len(out_shape) if isinstance(out_shape, list) else vmem(),
         compiler_params=pltpu.CompilerParams(vmem_limit_bytes=VMEM),
         name=name,
     )(*scalars, *arrays)
@@ -139,34 +139,55 @@
     return call(merge_kernel, "merge_keys", bf16(GROUPS, ROWS, KW), (zl,), landing, text, arrived)
 
 
-def attend_kernel(zl_ref, landing_ref, qdoc_ref, kdoc_ref, text_ref, two_ref, one_ref, own_ref, arrived_ref, out_ref):
+def prepare_kernel(
+    zl_ref, landing_ref, qdoc_ref, kdoc_ref, text_ref, two_ref, one_ref, own_ref,
+    query_ref, key_ref, value_ref, bias_ref,
+):
     present = landed(zl_ref[0] * ROWS, landing_ref[...])
     window = REACH + ROWS
     query_pos = lax.broadcasted_iota(jnp.int32, (ROWS, window), 0) + REACH
     key_pos = lax.broadcasted_iota(jnp.int32, (ROWS, window), 1)
     allowed = (kdoc_ref[...] == qdoc_ref[...]) & (key_pos <= query_pos)
+    bias_ref[...] = jnp.where(allowed, 0.0, -jnp.inf)
+    for group in range(GROUPS):
+        text = text_ref[group, :, :QW]
+        query_ref[group] = jnp.where(present, jnp.zeros_like(text), text)
+        for i, ref in enumerate((two_ref, one_ref, own_ref)):
+            span = slice(i * ROWS, (i + 1) * ROWS)
+            key_ref[group, :, span] = jnp.transpose(ref[group, :, :HD])
+            value_ref[group, span, :] = ref[group, :, HD:]
+
+
+def prepare(zl, *arrays):
+    window = REACH + ROWS
+    shapes = [
+        bf16(GROUPS, ROWS, QW),
+        bf16(GROUPS, HD, window),
+        bf16(GROUPS, window, HD),
+        jax.ShapeDtypeStruct((ROWS, window), jnp.float32),
+    ]
+    return call(prepare_kernel, "prepare", shapes, (zl,), *arrays)
+
+
+def attend_kernel(query_ref, key_ref, value_ref, bias_ref, arrived_ref, out_ref):
+    bias = bias_ref[...]
     factor = HD ** (-0.5)
     for group in range(GROUPS):
-        joined = jnp.concatenate([two_ref[group], one_ref[group], own_ref[group]], 0)
-        keys, values = joined[:, :HD], joined[:, HD:]
         queries = []
         for head in range(QPG):
             low = (head % 2) * HD
             arrived = arrived_ref[PLANE_OF[group * 2 + head // 2], :, low : low + HD]
-            text = text_ref[group, :, head * HD : (head + 1) * HD]
-            queries.append(jnp.where(present, arrived, text))
-        scores = lax.dot_general(
-            jnp.concatenate(queries, 0),
-            keys,
-            (((1,), (1,)), ((), ())),
-            preferred_element_type=jnp.float32,
+            queries.append(arrived + query_ref[group, :, head * HD : (head + 1) * HD])
+        scores = jnp.dot(
+            jnp.concatenate(queries, 0), key_ref[group], preferred_element_type=jnp.float32
         )
         for head in range(QPG):
-            masked = jnp.where(allowed, scores[head * ROWS : (head + 1) * ROWS] * factor, -jnp.inf)
+            masked = scores[head * ROWS : (head + 1) * ROWS] * factor + bias
             row_max = jnp.max(masked, axis=1, keepdims=True)
             terms = jnp.exp(masked - row_max)
             total = jnp.sum(terms, axis=1, keepdims=True)
-            summed = jnp.dot(terms.astype(jnp.bfloat16), values, preferred_element_type=jnp.float32)
+            weights = terms.astype(jnp.bfloat16)
+            summed = jnp.dot(weights, value_ref[group], preferred_element_type=jnp.float32)
             out_ref[group, :, head * HD : (head + 1) * HD] = (summed / total).astype(jnp.bfloat16)
 
 
@@ -234,10 +255,8 @@
     blocks_q = to_blocks([two_sources(each) for each in landings], slots_q)
     arrived_q = over_planes(after(blocks_q, two_kv))
 
-    out = call(
-        attend_kernel, "attend", bf16(GROUPS, ROWS, QW),
-        (zl_arr,), landing, qdoc, kdoc, text, two_kv, one_kv, own_kv, arrived_q,
-    )
+    ready = prepare(zl_arr, landing, qdoc, kdoc, text, two_kv, one_kv, own_kv)
+    out = call(attend_kernel, "attend", bf16(GROUPS, ROWS, QW), (), *ready, arrived_q)
     return jnp.transpose(out, (1, 0, 2))
 
 

time: 208 us -> 220 us (1.058)
  the two profiles are of different devices: /device:TPU:104 before, /device:TPU:1 now
where the time goes in v4:
time: 220 us; the launch traced here: 219 us
  waiting for transfers between devices  109 us (50%)
  starting transfers between devices  78.6 us (36%)
  local copies, waits for them, and re-layouts  14.4 us (7%)
  Pallas kernels  9.88 us (4%)
  other arithmetic  4.47 us (2%)
  between operations  2.3 us (1%)
    all_to_all x2, waiting for transfers between devices, over_planes(): lax.all_to_all(blocks, ('zh', 'zl'), split_axis=0, concat_axis=0, tiled=T...  77.1 us
    all_to_all x2, starting transfers between devices, over_planes(): lax.all_to_all(blocks, ('zh', 'zl'), split_axis=0, concat_axis=0, tiled=T...  30 us
    all_to_all x2, starting transfers between devices, over_columns(): lax.all_to_all(slots, ('x', 'y', 'c'), split_axis=0, concat_axis=0, tiled...  22.1 us
    ppermute x3, starting transfers between devices, from_behind(): lax.ppermute(value, AXES, [(i, i + steps) for i in range(COUNT - steps)])  15.3 us
    ppermute x2, waiting for transfers between devices, to_plane(): return lax.ppermute(value, AXES, ids)  11.9 us
    ppermute x2, starting transfers between devices, to_plane(): return lax.ppermute(value, AXES, ids)  11.2 us
    all_to_all x2, waiting for transfers between devices, over_columns(): lax.all_to_all(slots, ('x', 'y', 'c'), split_axis=0, concat_axis=0, tiled...  10.8 us
    unnamed x23, local copies, waits for them, and re-layouts  9.92 us
  transfers between devices with their start and end apart: 9, of which 8 were waited for; matrix products, arithmetic and copies ran while one was open for 2% of the time, Pallas kernels for 2%

profile of v4, /device:TPU:1, one launch (start us, length us, event | category | flops | bytes accessed | tf_op | source)
XLA Modules:
  0.0 219.1 jit_solution(12467841747113383069)
XLA Ops:
  5.8 1.2 to_slots.2
  7.1 10.4 %all-to-all-start = ((bf16[32,32,256]{2,1,0:T(8,128)(2,1)}), bf16[32,32,256]{2,1,0:T(8,128)(2,1)S(1)}, u32[]{:S(2)}, u32[]{:S(2)}) async-start(bf16[32,32,256]{2,1,0:T(8,128)(2,1)} %to_slots.2), calls=%async_computation | async-start | bytes 1048576 | tf_op jit(solution)/shard_map/all_to_all | solution.py:56
  17.5 9.3 %collective-permute-start.1 = (bf16[512,256]{1,0:T(8,128)(2,1)S(1)}, bf16[512,256]{1,0:T(8,128)(2,1)S(1)}, u32[]{:S(2)}, u32[]{:S(2)}) collective-permute-start(bf16[512,256]{1,0:T(8,128)(2,1)S(1)} %get-tuple-element.24), channel_id=1, source_target_pairs={{0,71},{1,3},{2,70},{3,2},{4,69},{5,64},{6,0},{7,6},{64,1},{65,66}... | collective-permute-start | bytes 786440 | tf_op jit(solution)/shard_map/ppermute | solution.py:48
  26.8 1.9 collective-permute-start.2
  28.8 2.3 %select_reduce_fusion = (s32[64,16]{1,0:T(8,128)S(1)}, s32[64,16]{1,0:T(8,128)S(1)}) fusion(s32[64,512]{1,0:T(8,128)S(1)} %get-tuple-element.30, s32[64,512]{1,0:T(8,128)S(1)} %get-tuple-element.28, s32[64,512]{1,0:T(8,128)S(1)} %get-tuple-element.31, s32[64,512]{1,0:T(8,128)S(1)} %get-tuple-element.29), kind=kLoop, calls=%fused_computation | loop fusion | flops 3143680 | bytes 532480 | tf_op jit(solution)/shard_map/reduce_sum | solution.py:229
  31.3 7.4 %collective-permute-done.1.refs_2_ = bf16[512,256]{1,0:T(8,128)(2,1)S(1)} collective-permute-done((bf16[512,256]{1,0:T(8,128)(2,1)S(1)}, bf16[512,256]{1,0:T(8,128)(2,1)S(1)}, u32[]{:S(2)}, u32[]{:S(2)}) %collective-permute-start.1) | collective-permute-done | bytes 262176 | tf_op jit(solution)/shard_map/ppermute | solution.py:48
  38.7 4.5 %collective-permute-done.2.refs_3_ = bf16[512,256]{1,0:T(8,128)(2,1)S(1)} collective-permute-done((bf16[512,256]{1,0:T(8,128)(2,1)S(1)}, bf16[512,256]{1,0:T(8,128)(2,1)S(1)}, u32[]{:S(2)}, u32[]{:S(2)}) %collective-permute-start.2) | collective-permute-done | bytes 262176 | tf_op jit(solution)/shard_map/ppermute | solution.py:48
  43.2 1.7 to_blocks.2
  44.9 19.4 %all-to-all-start.1 = ((bf16[16,128,256]{2,1,0:T(8,128)(2,1)}), bf16[16,128,256]{2,1,0:T(8,128)(2,1)S(1)}, u32[]{:S(2)}, u32[]{:S(2)}) async-start(bf16[16,128,256]{2,1,0:T(8,128)(2,1)} %to_blocks.2), calls=%async_computation.1 | async-start | bytes 2097152 | tf_op jit(solution)/shard_map/all_to_all | solution.py:60
  64.4 1.7 copy.22
  66.5 42.1 %all-to-all-done.1.arrived_ref = bf16[16,128,256]{2,1,0:T(8,128)(2,1)S(1)} async-done(((bf16[16,128,256]{2,1,0:T(8,128)(2,1)}), bf16[16,128,256]{2,1,0:T(8,128)(2,1)S(1)}, u32[]{:S(2)}, u32[]{:S(2)}) %all-to-all-start.1) | async-done | bytes 1048608 | tf_op jit(solution)/shard_map/all_to_all | solution.py:60
  108.7 4.1 %collective-permute-start.3 = (bf16[8,128,256]{2,1,0:T(8,128)(2,1)S(1)}, bf16[8,128,256]{2,1,0:T(8,128)(2,1)}, u32[]{:S(2)}, u32[]{:S(2)}) collective-permute-start(bf16[8,128,256]{2,1,0:T(8,128)(2,1)S(1)} %merge_keys.1.own_ref), channel_id=1, source_target_pairs={{0,1},{1,2},{2,3},{3,4},{4,5},{5,6},{6,7},{7,8},{8,9},{9,10},{10,1... | collective-permute-start | bytes 1572872 | tf_op jit(solution)/shard_map/ppermute | solution.py:52
  114.7 11.7 %all-to-all-start.2 = ((bf16[32,64,256]{2,1,0:T(8,128)(2,1)}), bf16[32,64,256]{2,1,0:T(8,128)(2,1)S(1)}, u32[]{:S(2)}, u32[]{:S(2)}) async-start(bf16[32,64,256]{2,1,0:T(8,128)(2,1)} %copy-done.1), calls=%async_computation.2 | async-start | bytes 2097152 | tf_op jit(solution)/shard_map/all_to_all | solution.py:56
  126.4 7.1 %collective-permute-done.3.one_ref = bf16[8,128,256]{2,1,0:T(8,128)(2,1)} collective-permute-done((bf16[8,128,256]{2,1,0:T(8,128)(2,1)S(1)}, bf16[8,128,256]{2,1,0:T(8,128)(2,1)}, u32[]{:S(2)}, u32[]{:S(2)}) %collective-permute-start.3) | collective-permute-done | bytes 524320 | tf_op jit(solution)/shard_map/ppermute | solution.py:52
  133.5 1.9 collective-permute-start.4
  135.7 10.8 %all-to-all-done.2.slots_ref = bf16[32,64,256]{2,1,0:T(8,128)(2,1)S(1)} async-done(((bf16[32,64,256]{2,1,0:T(8,128)(2,1)}), bf16[32,64,256]{2,1,0:T(8,128)(2,1)S(1)}, u32[]{:S(2)}, u32[]{:S(2)}) %all-to-all-start.2) | async-done | bytes 1048608 | tf_op jit(solution)/shard_map/all_to_all | solution.py:56
  146.5 1.3 to_blocks.3
  148.7 2.2 collective-permute-done.4.two_ref
  150.9 10.6 %all-to-all-start.3 = ((bf16[16,128,256]{2,1,0:T(8,128)(2,1)}), bf16[16,128,256]{2,1,0:T(8,128)(2,1)S(1)}, u32[]{:S(2)}, u32[]{:S(2)}) async-start(bf16[16,128,256]{2,1,0:T(8,128)(2,1)} %copy-done), calls=%async_computation.3 | async-start | bytes 2097152 | tf_op jit(solution)/shard_map/all_to_all | solution.py:60
  161.5 9.3 %collective-permute-start = (s32[256]{0:T(256)S(1)}, s32[256]{0:T(256)S(1)}, u32[]{:S(2)}, u32[]{:S(2)}) collective-permute-start(s32[256]{0:T(256)S(1)} %slice.24), channel_id=1, source_target_pairs={{0,8},{1,9},{2,10},{3,11},{4,12},{5,13},{6,14},{7,15},{8,16},{9,17... | collective-permute-start | bytes 3080 | tf_op jit(solution)/shard_map/ppermute | solution.py:52
  171.5 1.8 prepare.1
  176.0 35.0 %all-to-all-done.3.arrived_ref = bf16[16,128,256]{2,1,0:T(8,128)(2,1)S(1)} async-done(((bf16[16,128,256]{2,1,0:T(8,128)(2,1)}), bf16[16,128,256]{2,1,0:T(8,128)(2,1)S(1)}, u32[]{:S(2)}, u32[]{:S(2)}) %all-to-all-start.3) | async-done | bytes 1048608 | tf_op jit(solution)/shard_map/all_to_all | solution.py:60
  214.6 3.0 %attend.1 = bf16[8,128,512]{2,1,0:T(8,128)(2,1)S(1)} custom-call(bf16[8,128,512]{2,1,0:T(8,128)(2,1)S(1)} %copy-done.3, bf16[8,128,384]{2,1,0:T(8,128)(2,1)S(1)} %copy-done.5, bf16[8,384,128]{2,1,0:T(8,128)(2,1)S(1)} %copy-done.7, f32[128,384]{1,0:T(8,128)S(1)} %get-tuple-element.16.bias_ref, bf16[16,128,256]{2,1,0:T(8,128)(2,1)S(1)} %all-to-all-done.3.arrived_ref), custom_call_target="tpu_custom_call" | custom-call | tf_op jit(solution)/shard_map/attend/pallas_call | solution.py:76
  217.6 1.5 copy.20
  (56 shorter events, 14.5 us)
Async XLA Ops:
  7.1 36.1 %all-to-all-start = ((bf16[32,32,256]{2,1,0:T(8,128)(2,1)}), bf16[32,32,256]{2,1,0:T(8,128)(2,1)S(1)}, u32[]{:S(2)}, u32[]{:S(2)}) async-start(bf16[32,32,256]{2,1,0:T(8,128)(2,1)} %to_slots.2), calls=%async_computation | async-start | bytes 1048576 | tf_op jit(solution)/shard_map/all_to_all | solution.py:56
  17.5 21.2 %collective-permute-start.1 = (bf16[512,256]{1,0:T(8,128)(2,1)S(1)}, bf16[512,256]{1,0:T(8,128)(2,1)S(1)}, u32[]{:S(2)}, u32[]{:S(2)}) collective-permute-start(bf16[512,256]{1,0:T(8,128)(2,1)S(1)} %get-tuple-element.24), channel_id=1, source_target_pairs={{0,71},{1,3},{2,70},{3,2},{4,69},{5,64},{6,0},{7,6},{64,1},{65,66}... | collective-permute-start | bytes 786440 | tf_op jit(solution)/shard_map/ppermute | solution.py:48
  26.8 16.4 %collective-permute-start.2 = (bf16[512,256]{1,0:T(8,128)(2,1)S(1)}, bf16[512,256]{1,0:T(8,128)(2,1)S(1)}, u32[]{:S(2)}, u32[]{:S(2)}) collective-permute-start(bf16[512,256]{1,0:T(8,128)(2,1)S(1)} %get-tuple-element.22), channel_id=1, source_target_pairs={{0,1},{1,66},{2,65},{3,5},{4,7},{5,4},{6,67},{7,68},{64,71},{65,3}... | collective-permute-start | bytes 786440 | tf_op jit(solution)/shard_map/ppermute | solution.py:48
  43.2 1.7 copy-start.8
  44.9 63.7 %all-to-all-start.1 = ((bf16[16,128,256]{2,1,0:T(8,128)(2,1)}), bf16[16,128,256]{2,1,0:T(8,128)(2,1)S(1)}, u32[]{:S(2)}, u32[]{:S(2)}) async-start(bf16[16,128,256]{2,1,0:T(8,128)(2,1)} %to_blocks.2), calls=%async_computation.1 | async-start | bytes 2097152 | tf_op jit(solution)/shard_map/all_to_all | solution.py:60
  108.6 4.4 %copy-start.9 = (bf16[512,256]{1,0:T(8,128)(2,1)S(1)}, bf16[512,256]{1,0:T(8,128)(2,1)}, u32[]{:S(2)}) copy-start(bf16[512,256]{1,0:T(8,128)(2,1)} %copy-done.8) | copy-start | bytes 786436
  108.7 24.8 %collective-permute-start.3 = (bf16[8,128,256]{2,1,0:T(8,128)(2,1)S(1)}, bf16[8,128,256]{2,1,0:T(8,128)(2,1)}, u32[]{:S(2)}, u32[]{:S(2)}) collective-permute-start(bf16[8,128,256]{2,1,0:T(8,128)(2,1)S(1)} %merge_keys.1.own_ref), channel_id=1, source_target_pairs={{0,1},{1,2},{2,3},{3,4},{4,5},{5,6},{6,7},{7,8},{8,9},{9,10},{10,1... | collective-permute-start | bytes 1572872 | tf_op jit(solution)/shard_map/ppermute | solution.py:52
  113.7 1.0 copy-start.1
  114.7 31.8 %all-to-all-start.2 = ((bf16[32,64,256]{2,1,0:T(8,128)(2,1)}), bf16[32,64,256]{2,1,0:T(8,128)(2,1)S(1)}, u32[]{:S(2)}, u32[]{:S(2)}) async-start(bf16[32,64,256]{2,1,0:T(8,128)(2,1)} %copy-done.1), calls=%async_computation.2 | async-start | bytes 2097152 | tf_op jit(solution)/shard_map/all_to_all | solution.py:56
  133.5 17.4 %collective-permute-start.4 = (bf16[8,128,256]{2,1,0:T(8,128)(2,1)}, bf16[8,128,256]{2,1,0:T(8,128)(2,1)}, u32[]{:S(2)}, u32[]{:S(2)}) collective-permute-start(bf16[8,128,256]{2,1,0:T(8,128)(2,1)} %collective-permute-done.3.one_ref), channel_id=1, source_target_pairs={{0,1},{1,2},{2,3},{3,4},{4,5},{5,6},{6,7},{7,8},{8,9},{9,10},{10,1... | collective-permute-start | bytes 1572872 | tf_op jit(solution)/shard_map/ppermute | solution.py:52
  147.8 1.0 copy-start
  148.7 12.8 %copy-start.10 = (s32[1024]{0:T(1024)S(1)}, s32[1024]{0:T(1024)}, u32[]{:S(2)}) copy-start(s32[1024]{0:T(1024)} %param.8) | copy-start | bytes 12292
  150.9 60.2 %all-to-all-start.3 = ((bf16[16,128,256]{2,1,0:T(8,128)(2,1)}), bf16[16,128,256]{2,1,0:T(8,128)(2,1)S(1)}, u32[]{:S(2)}, u32[]{:S(2)}) async-start(bf16[16,128,256]{2,1,0:T(8,128)(2,1)} %copy-done), calls=%async_computation.3 | async-start | bytes 2097152 | tf_op jit(solution)/shard_map/all_to_all | solution.py:60
  161.5 9.8 %collective-permute-start = (s32[256]{0:T(256)S(1)}, s32[256]{0:T(256)S(1)}, u32[]{:S(2)}, u32[]{:S(2)}) collective-permute-start(s32[256]{0:T(256)S(1)} %slice.24), channel_id=1, source_target_pairs={{0,8},{1,9},{2,10},{3,11},{4,12},{5,13},{6,14},{7,15},{8,16},{9,17... | collective-permute-start | bytes 3080 | tf_op jit(solution)/shard_map/ppermute | solution.py:52
  173.2 1.0 copy-start.2
  174.2 0.9 copy-start.4
  175.1 0.9 copy-start.6
  211.1 1.2 copy-start.3
  212.3 1.1 copy-start.5
  213.4 1.1 copy-start.7

commit v5 on v3

--- a/solution.py
+++ b/solution.py
@@ -141,10 +141,11 @@
 
 def attend_kernel(zl_ref, landing_ref, qdoc_ref, kdoc_ref, text_ref, two_ref, one_ref, own_ref, arrived_ref, out_ref):
     present = landed(zl_ref[0] * ROWS, landing_ref[...])
-    window = REACH + ROWS
-    query_pos = lax.broadcasted_iota(jnp.int32, (ROWS, window), 0) + REACH
-    key_pos = lax.broadcasted_iota(jnp.int32, (ROWS, window), 1)
-    allowed = (kdoc_ref[...] == qdoc_ref[...]) & (key_pos <= query_pos)
+    row = lax.broadcasted_iota(jnp.int32, (ROWS, ROWS), 0)
+    lower = lax.broadcasted_iota(jnp.int32, (ROWS, ROWS), 1) <= row
+    qdoc, kdoc = qdoc_ref[...], kdoc_ref[...]
+    fold_ok = jnp.where(lower, kdoc[:, REACH:], kdoc[:, :ROWS]) == qdoc
+    one_ok = kdoc[:, ROWS:REACH] == qdoc
     factor = HD ** (-0.5)
     for group in range(GROUPS):
         joined = jnp.concatenate([two_ref[group], one_ref[group], own_ref[group]], 0)
@@ -162,11 +163,16 @@
             preferred_element_type=jnp.float32,
         )
         for head in range(QPG):
-            masked = jnp.where(allowed, scores[head * ROWS : (head + 1) * ROWS] * factor, -jnp.inf)
-            row_max = jnp.max(masked, axis=1, keepdims=True)
-            terms = jnp.exp(masked - row_max)
-            total = jnp.sum(terms, axis=1, keepdims=True)
-            summed = jnp.dot(terms.astype(jnp.bfloat16), values, preferred_element_type=jnp.float32)
+            block = scores[head * ROWS : (head + 1) * ROWS]
+            fold = jnp.where(lower, block[:, REACH:], block[:, :ROWS]) * factor
+            fold = jnp.where(fold_ok, fold, -jnp.inf)
+            one = jnp.where(one_ok, block[:, ROWS:REACH] * factor, -jnp.inf)
+            row_max = jnp.max(jnp.maximum(fold, one), axis=1, keepdims=True)
+            fold, one = jnp.exp(fold - row_max), jnp.exp(one - row_max)
+            total = jnp.sum(fold + one, axis=1, keepdims=True)
+            terms = [jnp.where(lower, 0.0, fold), one, jnp.where(lower, fold, 0.0)]
+            weights = jnp.concatenate(terms, 1).astype(jnp.bfloat16)
+            summed = jnp.dot(weights, values, preferred_element_type=jnp.float32)
             out_ref[group, :, head * HD : (head + 1) * HD] = (summed / total).astype(jnp.bfloat16)
 
 

time: 208 us -> 208 us (level)
  no operation moved by 1% of the time
where the time goes in v5:
time: 208 us; the launch traced here: 207 us
  waiting for transfers between devices  107 us (51%)
  starting transfers between devices  77.6 us (37%)
  Pallas kernels  10.3 us (5%)
  local copies, waits for them, and re-layouts  5.59 us (3%)
  other arithmetic  4.49 us (2%)
  between operations  2.25 us (1%)
    all_to_all x2, waiting for transfers between devices, over_planes(): lax.all_to_all(blocks, ('zh', 'zl'), split_axis=0, concat_axis=0, tiled=T...  86.5 us
    all_to_all x2, starting transfers between devices, over_planes(): lax.all_to_all(blocks, ('zh', 'zl'), split_axis=0, concat_axis=0, tiled=T...  38.1 us
    all_to_all x2, starting transfers between devices, over_columns(): lax.all_to_all(slots, ('x', 'y', 'c'), split_axis=0, concat_axis=0, tiled...  14.4 us
    ppermute x2, starting transfers between devices, to_plane(): return lax.ppermute(value, AXES, ids)  14.1 us
    ppermute x3, starting transfers between devices, from_behind(): lax.ppermute(value, AXES, [(i, i + steps) for i in range(COUNT - steps)])  11 us
    pallas_call x6, Pallas kernels, call(): pl.pallas_call(kernel, out_shape=out_shape, in_specs=[smem()] * len(scala...  10.3 us
    ppermute x2, waiting for transfers between devices, to_plane(): return lax.ppermute(value, AXES, ids)  7.93 us
    all_to_all x2, waiting for transfers between devices, over_columns(): lax.all_to_all(slots, ('x', 'y', 'c'), split_axis=0, concat_axis=0, tiled...  7.9 us
  transfers between devices with their start and end apart: 9, of which 6 were waited for; matrix products, arithmetic and copies ran while one was open for 3% of the time, Pallas kernels for 2%

profile of v5, /device:TPU:104, one launch (start us, length us, event | category | flops | bytes accessed | tf_op | source)
XLA Modules:
  0.0 206.8 jit_solution(9548600403720115959)
XLA Ops:
  0.0 1.2 broadcast_select_fusion
  1.2 2.0 collective-permute-start.1
  3.2 12.1 %collective-permute-start.2 = (bf16[512,256]{1,0:T(8,128)(2,1)S(1)}, bf16[512,256]{1,0:T(8,128)(2,1)S(1)}, u32[]{:S(2)}, u32[]{:S(2)}) collective-permute-start(bf16[512,256]{1,0:T(8,128)(2,1)S(1)} %get-tuple-element.14), channel_id=1, source_target_pairs={{0,1},{1,66},{2,65},{3,5},{4,7},{5,4},{6,67},{7,68},{64,71},{65,3}... | collective-permute-start | bytes 786440 | tf_op jit(solution)/shard_map/ppermute | solution.py:48
  18.5 1.2 to_slots.2
  19.7 7.5 %all-to-all-start = ((bf16[32,32,256]{2,1,0:T(8,128)(2,1)}), bf16[32,32,256]{2,1,0:T(8,128)(2,1)S(1)}, u32[]{:S(2)}, u32[]{:S(2)}) async-start(bf16[32,32,256]{2,1,0:T(8,128)(2,1)} %to_slots.2), calls=%async_computation | async-start | bytes 1048576 | tf_op jit(solution)/shard_map/all_to_all | solution.py:56
  27.3 2.2 %select_reduce_fusion = (s32[64,16]{1,0:T(8,128)S(1)}, s32[64,16]{1,0:T(8,128)S(1)}) fusion(s32[64,512]{1,0:T(8,128)S(1)} %get-tuple-element.22, s32[64,512]{1,0:T(8,128)S(1)} %get-tuple-element.20, s32[64,512]{1,0:T(8,128)S(1)} %get-tuple-element.23, s32[64,512]{1,0:T(8,128)S(1)} %get-tuple-element.21), kind=kLoop, calls=%fused_computation | loop fusion | flops 3143680 | bytes 532480 | tf_op jit(solution)/shard_map/reduce_sum | solution.py:214
  29.8 7.9 %collective-permute-done.2.refs_3_ = bf16[512,256]{1,0:T(8,128)(2,1)S(1)} collective-permute-done((bf16[512,256]{1,0:T(8,128)(2,1)S(1)}, bf16[512,256]{1,0:T(8,128)(2,1)S(1)}, u32[]{:S(2)}, u32[]{:S(2)}) %collective-permute-start.2) | collective-permute-done | bytes 262176 | tf_op jit(solution)/shard_map/ppermute | solution.py:48
  37.7 1.7 to_blocks.2
  39.4 10.4 %all-to-all-start.1 = ((bf16[16,128,256]{2,1,0:T(8,128)(2,1)}), bf16[16,128,256]{2,1,0:T(8,128)(2,1)S(1)}, u32[]{:S(2)}, u32[]{:S(2)}) async-start(bf16[16,128,256]{2,1,0:T(8,128)(2,1)} %to_blocks.2), calls=%async_computation.1 | async-start | bytes 2097152 | tf_op jit(solution)/shard_map/all_to_all | solution.py:60
  50.0 1.7 copy.22
  52.0 45.8 %all-to-all-done.1.arrived_ref = bf16[16,128,256]{2,1,0:T(8,128)(2,1)S(1)} async-done(((bf16[16,128,256]{2,1,0:T(8,128)(2,1)}), bf16[16,128,256]{2,1,0:T(8,128)(2,1)S(1)}, u32[]{:S(2)}, u32[]{:S(2)}) %all-to-all-start.1) | async-done | bytes 1048608 | tf_op jit(solution)/shard_map/all_to_all | solution.py:60
  98.0 3.2 %collective-permute-start.3 = (bf16[8,128,256]{2,1,0:T(8,128)(2,1)S(1)}, bf16[8,128,256]{2,1,0:T(8,128)(2,1)}, u32[]{:S(2)}, u32[]{:S(2)}) collective-permute-start(bf16[8,128,256]{2,1,0:T(8,128)(2,1)S(1)} %merge_keys.1.own_ref), channel_id=1, source_target_pairs={{0,1},{1,2},{2,3},{3,4},{4,5},{5,6},{6,7},{7,8},{8,9},{9,10},{10,1... | collective-permute-start | bytes 1572872 | tf_op jit(solution)/shard_map/ppermute | solution.py:52
  102.0 1.0 copy-done
  102.9 6.9 %all-to-all-start.2 = ((bf16[32,64,256]{2,1,0:T(8,128)(2,1)}), bf16[32,64,256]{2,1,0:T(8,128)(2,1)S(1)}, u32[]{:S(2)}, u32[]{:S(2)}) async-start(bf16[32,64,256]{2,1,0:T(8,128)(2,1)} %copy-done), calls=%async_computation.2 | async-start | bytes 2097152 | tf_op jit(solution)/shard_map/all_to_all | solution.py:56
  109.8 1.7 collective-permute-done.3.one_ref
  111.5 5.7 %collective-permute-start.4 = (bf16[8,128,256]{2,1,0:T(8,128)(2,1)}, bf16[8,128,256]{2,1,0:T(8,128)(2,1)}, u32[]{:S(2)}, u32[]{:S(2)}) collective-permute-start(bf16[8,128,256]{2,1,0:T(8,128)(2,1)} %collective-permute-done.3.one_ref), channel_id=1, source_target_pairs={{0,1},{1,2},{2,3},{3,4},{4,5},{5,6},{6,7},{7,8},{8,9},{9,10},{10,1... | collective-permute-start | bytes 1572872 | tf_op jit(solution)/shard_map/ppermute | solution.py:52
  117.5 7.9 %all-to-all-done.2.slots_ref = bf16[32,64,256]{2,1,0:T(8,128)(2,1)S(1)} async-done(((bf16[32,64,256]{2,1,0:T(8,128)(2,1)}), bf16[32,64,256]{2,1,0:T(8,128)(2,1)S(1)}, u32[]{:S(2)}, u32[]{:S(2)}) %all-to-all-start.2) | async-done | bytes 1048608 | tf_op jit(solution)/shard_map/all_to_all | solution.py:56
  125.4 2.2 %to_blocks.3 = bf16[16,128,256]{2,1,0:T(8,128)(2,1)} custom-call(s32[1,1024]{1,0:T(1,128)S(1)} %reshape.177.low_land, s32[1,1024]{1,0:T(1,128)S(1)} %reshape.178.high_land, bf16[32,64,256]{2,1,0:T(8,128)(2,1)S(1)} %all-to-all-done.2.slots_ref), custom_call_target="tpu_custom_call" | custom-call | tf_op jit(solution)/shard_map/to_blocks/pallas_call | solution.py:76
  127.6 27.7 %all-to-all-start.3 = ((bf16[16,128,256]{2,1,0:T(8,128)(2,1)}), bf16[16,128,256]{2,1,0:T(8,128)(2,1)S(1)}, u32[]{:S(2)}, u32[]{:S(2)}) async-start(bf16[16,128,256]{2,1,0:T(8,128)(2,1)} %to_blocks.3), calls=%async_computation.3 | async-start | bytes 2097152 | tf_op jit(solution)/shard_map/all_to_all | solution.py:60
  155.4 2.1 %collective-permute-start = (s32[256]{0:T(256)S(1)}, s32[256]{0:T(256)S(1)}, u32[]{:S(2)}, u32[]{:S(2)}) collective-permute-start(s32[256]{0:T(256)S(1)} %slice.24), channel_id=1, source_target_pairs={{0,8},{1,9},{2,10},{3,11},{4,12},{5,13},{6,14},{7,15},{8,16},{9,17... | collective-permute-start | bytes 3080 | tf_op jit(solution)/shard_map/ppermute | solution.py:52
  157.7 2.6 %collective-permute-done = s32[256]{0:T(256)S(1)} collective-permute-done((s32[256]{0:T(256)S(1)}, s32[256]{0:T(256)S(1)}, u32[]{:S(2)}, u32[]{:S(2)}) %collective-permute-start) | collective-permute-done | bytes 1056 | tf_op jit(solution)/shard_map/ppermute | solution.py:52
  160.3 40.7 %all-to-all-done.3.arrived_ref = bf16[16,128,256]{2,1,0:T(8,128)(2,1)S(1)} async-done(((bf16[16,128,256]{2,1,0:T(8,128)(2,1)}), bf16[16,128,256]{2,1,0:T(8,128)(2,1)S(1)}, u32[]{:S(2)}, u32[]{:S(2)}) %all-to-all-start.3) | async-done | bytes 1048608 | tf_op jit(solution)/shard_map/all_to_all | solution.py:60
  201.0 4.3 %attend.1 = bf16[8,128,512]{2,1,0:T(8,128)(2,1)S(1)} custom-call(s32[1]{0:T(128)} %bitcast.zl_ref, s32[1,1024]{1,0:T(1,128)S(1)} %reshape.173.landing_ref, s32[128,1]{1,0:T(8,128)S(1)} %copy.19.qdoc_ref, s32[1,384]{1,0:T(1,128)S(1)} %reshape.175.kdoc_ref, bf16[8,128,768]{2,1,0:T(8,128)(2,1)S(1)} %bitcast.30, ...), custom_call_target="tpu_custom_call" | custom-call | tf_op jit(solution)/shard_map/attend/pallas_call | solution.py:76
  205.3 1.5 copy.20
  (45 shorter events, 3.3 us)
Async XLA Ops:
  0.0 15.4 %copy-start.5 = (s32[16]{0:T(128)S(1)}, s32[16]{0:T(128)}, u32[]{:S(2)}) copy-start(s32[16]{0:T(128)} %constant.167.clone) | copy-start | bytes 196
  0.0 18.0 %copy-start.3 = (s32[32768]{0:T(1024)S(1)}, s32[32768]{0:T(1024)}, u32[]{:S(2)}) copy-start(s32[32768]{0:T(1024)} %param.7) | copy-start | bytes 393220
  1.2 28.6 %collective-permute-start.1 = (bf16[512,256]{1,0:T(8,128)(2,1)S(1)}, bf16[512,256]{1,0:T(8,128)(2,1)S(1)}, u32[]{:S(2)}, u32[]{:S(2)}) collective-permute-start(bf16[512,256]{1,0:T(8,128)(2,1)S(1)} %get-tuple-element.16), channel_id=1, source_target_pairs={{0,71},{1,3},{2,70},{3,2},{4,69},{5,64},{6,0},{7,6},{64,1},{65,66}... | collective-permute-start | bytes 786440 | tf_op jit(solution)/shard_map/ppermute | solution.py:48
  3.2 34.5 %collective-permute-start.2 = (bf16[512,256]{1,0:T(8,128)(2,1)S(1)}, bf16[512,256]{1,0:T(8,128)(2,1)S(1)}, u32[]{:S(2)}, u32[]{:S(2)}) collective-permute-start(bf16[512,256]{1,0:T(8,128)(2,1)S(1)} %get-tuple-element.14), channel_id=1, source_target_pairs={{0,1},{1,66},{2,65},{3,5},{4,7},{5,4},{6,67},{7,68},{64,71},{65,3}... | collective-permute-start | bytes 786440 | tf_op jit(solution)/shard_map/ppermute | solution.py:48
  19.7 18.0 %all-to-all-start = ((bf16[32,32,256]{2,1,0:T(8,128)(2,1)}), bf16[32,32,256]{2,1,0:T(8,128)(2,1)S(1)}, u32[]{:S(2)}, u32[]{:S(2)}) async-start(bf16[32,32,256]{2,1,0:T(8,128)(2,1)} %to_slots.2), calls=%async_computation | async-start | bytes 1048576 | tf_op jit(solution)/shard_map/all_to_all | solution.py:56
  37.7 1.7 copy-start.1
  39.4 58.4 %all-to-all-start.1 = ((bf16[16,128,256]{2,1,0:T(8,128)(2,1)}), bf16[16,128,256]{2,1,0:T(8,128)(2,1)S(1)}, u32[]{:S(2)}, u32[]{:S(2)}) async-start(bf16[16,128,256]{2,1,0:T(8,128)(2,1)} %to_blocks.2), calls=%async_computation.1 | async-start | bytes 2097152 | tf_op jit(solution)/shard_map/all_to_all | solution.py:60
  97.8 3.4 %copy-start.2 = (bf16[512,256]{1,0:T(8,128)(2,1)S(1)}, bf16[512,256]{1,0:T(8,128)(2,1)}, u32[]{:S(2)}) copy-start(bf16[512,256]{1,0:T(8,128)(2,1)} %copy-done.1) | copy-start | bytes 786436
  98.0 13.5 %collective-permute-start.3 = (bf16[8,128,256]{2,1,0:T(8,128)(2,1)S(1)}, bf16[8,128,256]{2,1,0:T(8,128)(2,1)}, u32[]{:S(2)}, u32[]{:S(2)}) collective-permute-start(bf16[8,128,256]{2,1,0:T(8,128)(2,1)S(1)} %merge_keys.1.own_ref), channel_id=1, source_target_pairs={{0,1},{1,2},{2,3},{3,4},{4,5},{5,6},{6,7},{7,8},{8,9},{9,10},{10,1... | collective-permute-start | bytes 1572872 | tf_op jit(solution)/shard_map/ppermute | solution.py:52
  102.0 1.0 copy-start
  102.9 22.4 %all-to-all-start.2 = ((bf16[32,64,256]{2,1,0:T(8,128)(2,1)}), bf16[32,64,256]{2,1,0:T(8,128)(2,1)S(1)}, u32[]{:S(2)}, u32[]{:S(2)}) async-start(bf16[32,64,256]{2,1,0:T(8,128)(2,1)} %copy-done), calls=%async_computation.2 | async-start | bytes 2097152 | tf_op jit(solution)/shard_map/all_to_all | solution.py:56
  111.5 16.1 %collective-permute-start.4 = (bf16[8,128,256]{2,1,0:T(8,128)(2,1)}, bf16[8,128,256]{2,1,0:T(8,128)(2,1)}, u32[]{:S(2)}, u32[]{:S(2)}) collective-permute-start(bf16[8,128,256]{2,1,0:T(8,128)(2,1)} %collective-permute-done.3.one_ref), channel_id=1, source_target_pairs={{0,1},{1,2},{2,3},{3,4},{4,5},{5,6},{6,7},{7,8},{8,9},{9,10},{10,1... | collective-permute-start | bytes 1572872 | tf_op jit(solution)/shard_map/ppermute | solution.py:52
  127.6 27.7 %copy-start.4 = (s32[1024]{0:T(1024)S(1)}, s32[1024]{0:T(1024)}, u32[]{:S(2)}) copy-start(s32[1024]{0:T(1024)} %param.8) | copy-start | bytes 12292
  127.6 73.4 %all-to-all-start.3 = ((bf16[16,128,256]{2,1,0:T(8,128)(2,1)}), bf16[16,128,256]{2,1,0:T(8,128)(2,1)S(1)}, u32[]{:S(2)}, u32[]{:S(2)}) async-start(bf16[16,128,256]{2,1,0:T(8,128)(2,1)} %to_blocks.3), calls=%async_computation.3 | async-start | bytes 2097152 | tf_op jit(solution)/shard_map/all_to_all | solution.py:60
  155.4 4.9 %collective-permute-start = (s32[256]{0:T(256)S(1)}, s32[256]{0:T(256)S(1)}, u32[]{:S(2)}, u32[]{:S(2)}) collective-permute-start(s32[256]{0:T(256)S(1)} %slice.24), channel_id=1, source_target_pairs={{0,8},{1,9},{2,10},{3,11},{4,12},{5,13},{6,14},{7,15},{8,16},{9,17... | collective-permute-start | bytes 3080 | tf_op jit(solution)/shard_map/ppermute | solution.py:52
